TPU v7x, 128 devices: a whole 4x4x4 slice. The times are simulated.
128 devices in a mesh: clus: 8 (over x, core), grp: 16 (over z, y).
Axes of the slice: x: 4, y: 4, z: 4, core: 2. Of those that a mesh axis runs over, the one named last changes fastest.
Arguments:
- embeddings: bfloat16 [262144, 1024], P(('clus', 'grp')), may hold values from -6 to 6
- labels: int32 [262144], P(('clus', 'grp')), may hold values from 0 to 3
- partner_block: int32 [128, 24], P(('clus', 'grp')), may hold values from 0 to 3
- own_block: int32 [128, 24], P(('clus', 'grp')), may hold values from 0 to 3
- live: int32 [128, 24], P(('clus', 'grp')), may hold values from 0 to 1, as said below
Outputs:
- best_similarity: float32 [262144], P(('clus', 'grp'))
Inputs may be any that keep to these rules, and one draw needn't show every extreme that they name: live is 0 or 1; each device draws k from 1 to 4 and each of its slots is live with probability k / 4; one device of the whole mesh has every slot live.
All inputs are finite; a program needn't handle non-finite values.
Results may differ from a plain program's by a relative error of at most 0.0014.
Values may be sent and summed in bfloat16 or wider, within the bound.
A program may use at most 128 MiB of HBM per device.

v0:
```python
import jax
import jax.numpy as jnp
from jax import lax
from jax.sharding import PartitionSpec as P

BLOCK = 512
PIECE = 512


EPS = 1e-06
FILL = -1.0


def normalize_rows(embeddings):
    widened = embeddings.astype(jnp.float32)
    inverse = lax.rsqrt(jnp.sum(widened * widened, axis=1, keepdims=True) + EPS)
    return (widened * inverse).astype(jnp.bfloat16)


def score_pair(own_rows, own_ids, own_labs, part_rows, part_ids, part_labs, active):
    cosine = jnp.dot(own_rows, part_rows.T, preferred_element_type=jnp.float32)
    keep_mask = (
        (own_labs[:, None] == part_labs[None, :])
        & (own_ids[:, None] != part_ids[None, :])
        & (active > 0)
    )
    scored = jnp.where(keep_mask, cosine, FILL)
    return (jnp.max(scored, axis=1), jnp.max(scored, axis=0))


def guarded_pair(own_rows, own_ids, own_labs, part_rows, part_ids, part_labs, active):
    return score_pair(own_rows, own_ids, own_labs, part_rows, part_ids, part_labs, active)


def raise_rows(best_now, values, anchor):
    length = values.shape[0]
    current = lax.dynamic_slice_in_dim(best_now, anchor, length, 0)
    return lax.dynamic_update_slice_in_dim(best_now, jnp.maximum(current, values), anchor, 0)


def spread_table(values, chosen, row_count):
    length = values.shape[1]
    owners = jnp.arange(row_count, dtype=jnp.int32) // length
    matched = owners[None, :] == chosen[:, None]
    return jnp.where(matched, jnp.tile(values, (1, row_count // length)), FILL)


def local_pairs(best_sim, normed, row_ids, labels, arrived, own_picks, actives):

    def visit(best_now, members):
        part_rows, part_ids, part_labs, chosen, active = members
        anchor = chosen * BLOCK
        own_rows = lax.dynamic_slice_in_dim(normed, anchor, BLOCK, 0)
        own_ids = lax.dynamic_slice_in_dim(row_ids, anchor, BLOCK, 0)
        own_labs = lax.dynamic_slice_in_dim(labels, anchor, BLOCK, 0)
        row_best, col_best = guarded_pair(
            own_rows, own_ids, own_labs, part_rows, part_ids, part_labs, active
        )
        return (raise_rows(best_now, row_best, anchor), col_best)

    return lax.scan(visit, best_sim, (arrived[0], arrived[1], arrived[2], own_picks, actives))


def on_device(embeddings, labels, partner_block, own_block, live):
    row_count = embeddings.shape[0]
    width = embeddings.shape[1]
    normed = normalize_rows(embeddings)
    clus_count = lax.axis_size("clus")
    grp_count = lax.axis_size("grp")
    first_id = (lax.axis_index("clus") * grp_count + lax.axis_index("grp")) * row_count
    row_ids = first_id + jnp.arange(row_count, dtype=jnp.int32)
    piece_rows = normed.reshape(row_count // PIECE, PIECE, width)
    piece_ids = row_ids.reshape(row_count // PIECE, PIECE)
    piece_labs = labels.reshape(row_count // PIECE, PIECE)
    best_sim = jnp.full((row_count,), FILL, jnp.float32)
    wanted = partner_block[0, :clus_count]
    asked = lax.all_to_all(
        wanted.reshape(clus_count, 1), "clus", split_axis=0, concat_axis=0, tiled=True
    )[:, 0]
    arrived = (
        lax.all_to_all(piece_rows[asked], "clus", split_axis=0, concat_axis=0, tiled=True),
        lax.all_to_all(piece_ids[asked], "clus", split_axis=0, concat_axis=0, tiled=True),
        lax.all_to_all(piece_labs[asked], "clus", split_axis=0, concat_axis=0, tiled=True),
    )
    best_sim, col_best = local_pairs(
        best_sim, normed, row_ids, labels, arrived, own_block[0, :clus_count], live[0, :clus_count]
    )
    returned = lax.all_to_all(col_best, "clus", split_axis=0, concat_axis=0, tiled=True)
    best_sim = jnp.maximum(best_sim, jnp.max(spread_table(returned, asked, row_count), axis=0))
    grp_wanted = partner_block[0, clus_count:]
    grp_picks = own_block[0, clus_count:]
    grp_actives = live[0, clus_count:]
    grp_asked = lax.all_to_all(
        grp_wanted.reshape(grp_count, 1), "grp", split_axis=0, concat_axis=0, tiled=True
    )[:, 0]
    grp_arrived = (
        lax.all_to_all(piece_rows[grp_asked], "grp", split_axis=0, concat_axis=0, tiled=True),
        lax.all_to_all(piece_ids[grp_asked], "grp", split_axis=0, concat_axis=0, tiled=True),
        lax.all_to_all(piece_labs[grp_asked], "grp", split_axis=0, concat_axis=0, tiled=True),
    )
    best_sim, grp_cols = local_pairs(
        best_sim, normed, row_ids, labels, grp_arrived, grp_picks, grp_actives
    )
    grp_returned = lax.all_to_all(grp_cols, "grp", split_axis=0, concat_axis=0, tiled=True)
    best_sim = jnp.maximum(
        best_sim, jnp.max(spread_table(grp_returned, grp_asked, row_count), axis=0)
    )
    return best_sim


def solution(mesh):
    placed = (
        P(("clus", "grp"), None),
        P(("clus", "grp")),
        P(("clus", "grp"), None),
        P(("clus", "grp"), None),
        P(("clus", "grp"), None),
    )
    return jax.shard_map(
        on_device, mesh=mesh, in_specs=placed, out_specs=P(("clus", "grp")), check_vma=False
    )
```

profile of v0, /device:TPU:1, one launch (start us, length us, event | category | flops | bytes accessed | tf_op | source)
XLA Modules:
  0.0 580.0 jit_solution(12401280864692448477)
XLA Ops:
  0.0 0.7 slice_bitcast_fusion.4
  0.7 0.7 copy.18
  1.3 5.8 %all-to-all-start = ((s32[8,1,1]{2,1,0:T(1,128)}), s32[8,1,1]{2,1,0:T(1,128)S(1)}, u32[]{:S(2)}, u32[]{:S(2)}) async-start(s32[8,1,1]{2,1,0:T(1,128)} %copy.18), calls=%async_computation | async-start | bytes 8192 | tf_op jit(solution)/shard_map/all_to_all | solution.py:77
  7.1 0.7 slice_bitcast_fusion.1
  7.9 3.1 fusion.8
  11.0 0.7 reshape.163
  11.7 0.7 copy.21
  12.3 7.8 %all-to-all-start.5 = ((s32[16,1,1]{2,1,0:T(1,128)}), s32[16,1,1]{2,1,0:T(1,128)S(1)}, u32[]{:S(2)}, u32[]{:S(2)}) async-start(s32[16,1,1]{2,1,0:T(1,128)} %copy.21), calls=%async_computation.5 | async-start | bytes 16384 | tf_op jit(solution)/shard_map/all_to_all | solution.py:93
  20.9 0.6 copy.20
  22.1 0.6 copy.19
  22.7 3.7 all-to-all-done.5
  26.5 6.2 %all-to-all-start.2 = ((s32[8,1,512]{2,1,0:T(1,128)}), s32[8,1,512]{2,1,0:T(1,128)S(1)}, u32[]{:S(2)}, u32[]{:S(2)}) async-start(s32[8,1,512]{2,1,0:T(1,128)} %copy.20), calls=%async_computation.2 | async-start | bytes 32768 | tf_op jit(solution)/shard_map/all_to_all | solution.py:82
  33.1 4.3 all-to-all-done.2
  37.3 3.9 all-to-all-start.1
  41.9 0.6 copy.23
  42.5 3.4 all-to-all-done.1
  45.9 3.5 all-to-all-start.7
  49.4 5.0 fusion.9
  54.4 6.8 %gather_fusion.2 = bf16[8,512,1024]{2,1,0:T(8,128)(2,1)} fusion(bf16[4,512,1024]{2,1,0:T(8,128)(2,1)} %bitcast.91, s32[1024]{0:T(1024)S(1)} %pad_clamp_fusion.1), kind=kCustom, calls=%fused_computation.2 | custom fusion | bytes 16777248 | tf_op jit(solution)/shard_map/gather | solution.py:81
  61.2 5.6 all-to-all-start.3
  67.4 0.7 copy.22
  68.1 92.6 %all-to-all-done.3 = bf16[8,512,1024]{2,1,0:T(8,128)(2,1)} async-done(((bf16[8,512,1024]{2,1,0:T(8,128)(2,1)}), bf16[8,512,1024]{2,1,0:T(8,128)(2,1)}, u32[]{:S(2)}, u32[]{:S(2)}) %all-to-all-start.3) | async-done | bytes 8388640 | tf_op jit(solution)/shard_map/all_to_all | solution.py:81
  160.7 6.9 %all-to-all-start.6 = ((s32[16,1,512]{2,1,0:T(1,128)}), s32[16,1,512]{2,1,0:T(1,128)S(1)}, u32[]{:S(2)}, u32[]{:S(2)}) async-start(s32[16,1,512]{2,1,0:T(1,128)} %copy.22), calls=%async_computation.6 | async-start | bytes 65536 | tf_op jit(solution)/shard_map/all_to_all | solution.py:99
  167.6 42.8 %while.24 = (s32[]{:T(128)}, f32[2048]{0:T(1024)S(1)}, f32[8,512]{1,0:T(8,128)S(1)}, s32[8]{0:T(128)S(1)}, s32[2048]{0:T(1024)S(1)}, /*index=5*/s32[8,512]{1,0:T...) while((s32[]{:T(128)}, f32[2048]{0:T(1024)S(1)}, ...), condition=%wide.region_4.5_spmd, body=%wide.region_1.4_spmd.sunk | while | flops 538705408 | bytes 2137340 | solution.py:61
  170.2 2.5 fusion.18
  175.6 2.5 fusion.18
  180.9 2.5 fusion.18
  186.3 2.5 fusion.18
  191.6 2.5 fusion.18
  197.0 2.5 fusion.18
  202.3 2.5 fusion.18
  207.7 2.5 fusion.18
  210.4 0.6 all_to_all.76
  211.0 4.4 all-to-all-start.4
  215.4 9.2 %gather_fusion.5 = bf16[16,512,1024]{2,1,0:T(8,128)(2,1)} fusion(bf16[4,512,1024]{2,1,0:T(8,128)(2,1)} %bitcast.92, s32[1024]{0:T(1024)S(1)} %pad_clamp_fusion), kind=kCustom, calls=%fused_computation.5 | custom fusion | bytes 33554496 | tf_op jit(solution)/shard_map/gather | solution.py:97
  224.6 7.1 %all-to-all-start.8 = ((bf16[16,512,1024]{2,1,0:T(8,128)(2,1)}), bf16[16,512,1024]{2,1,0:T(8,128)(2,1)}, u32[]{:S(2)}, u32[]{:S(2)}) async-start(bf16[16,512,1024]{2,1,0:T(8,128)(2,1)} %gather_fusion.5), calls=%async_computation.8 | async-start | bytes 33554432 | tf_op jit(solution)/shard_map/all_to_all | solution.py:97
  232.0 251.7 %all-to-all-done.8 = bf16[16,512,1024]{2,1,0:T(8,128)(2,1)} async-done(((bf16[16,512,1024]{2,1,0:T(8,128)(2,1)}), bf16[16,512,1024]{2,1,0:T(8,128)(2,1)}, u32[]{:S(2)}, u32[]{:S(2)}) %all-to-all-start.8) | async-done | bytes 16777248 | tf_op jit(solution)/shard_map/all_to_all | solution.py:97
  483.7 86.6 %while.25 = (s32[]{:T(128)}, f32[2048]{0:T(1024)S(1)}, f32[16,512]{1,0:T(8,128)S(1)}, s32[16]{0:T(128)S(1)}, s32[2048]{0:T(1024)S(1)}, /*index=5*/s32[16,512]{1,...) while((s32[]{:T(128)}, f32[2048]{0:T(1024)S(1)}, ...), condition=%wide.region_9.10_spmd, body=%wide.region_6.9_spmd.sunk | while | flops 538705408 | bytes 2137340 | solution.py:61
  483.7 0.6 dynamic_slice.114
  485.1 0.6 dynamic_slice.115
  486.3 2.5 fusion.19
  491.7 2.5 fusion.19
  497.2 2.5 fusion.19
  499.9 0.6 dynamic_slice.114
  501.3 0.6 dynamic_slice.115
  502.6 2.5 fusion.19
  505.3 0.6 dynamic_slice.114
  506.7 0.6 dynamic_slice.115
  508.0 2.5 fusion.19
  510.7 0.6 dynamic_slice.114
  512.1 0.6 dynamic_slice.115
  513.4 2.5 fusion.19
  517.6 0.6 dynamic_slice.115
  518.8 2.5 fusion.19
  524.2 2.5 fusion.19
  529.6 2.5 fusion.19
  535.0 2.5 fusion.19
  540.4 2.5 fusion.19
  545.9 2.5 fusion.19
  551.3 2.5 fusion.19
  556.7 2.5 fusion.19
  562.1 2.5 fusion.19
  567.5 2.5 fusion.19
  570.3 9.0 %all_to_all.100 = f32[16,1,512]{2,1,0:T(1,128)S(1)} all-to-all(f32[16,1,512]{2,1,0:T(1,128)S(1)} %all_to_all.88), channel_id=1, replica_groups=mesh['clus'=8,'grp'=16] {'grp'}, dimensions={0} | all-to-all | bytes 65536 | tf_op jit(solution)/shard_map/all_to_all | solution.py:104
  (201 shorter events, 37.3 us)
Async XLA Ops:
  1.3 11.0 %all-to-all-start = ((s32[8,1,1]{2,1,0:T(1,128)}), s32[8,1,1]{2,1,0:T(1,128)S(1)}, u32[]{:S(2)}, u32[]{:S(2)}) async-start(s32[8,1,1]{2,1,0:T(1,128)} %copy.18), calls=%async_computation | async-start | bytes 8192 | tf_op jit(solution)/shard_map/all_to_all | solution.py:77
  12.3 14.1 %all-to-all-start.5 = ((s32[16,1,1]{2,1,0:T(1,128)}), s32[16,1,1]{2,1,0:T(1,128)S(1)}, u32[]{:S(2)}, u32[]{:S(2)}) async-start(s32[16,1,1]{2,1,0:T(1,128)} %copy.21), calls=%async_computation.5 | async-start | bytes 16384 | tf_op jit(solution)/shard_map/all_to_all | solution.py:93
  26.5 10.9 %all-to-all-start.2 = ((s32[8,1,512]{2,1,0:T(1,128)}), s32[8,1,512]{2,1,0:T(1,128)S(1)}, u32[]{:S(2)}, u32[]{:S(2)}) async-start(s32[8,1,512]{2,1,0:T(1,128)} %copy.20), calls=%async_computation.2 | async-start | bytes 32768 | tf_op jit(solution)/shard_map/all_to_all | solution.py:82
  37.3 8.6 %all-to-all-start.1 = ((s32[8,1,512]{2,1,0:T(1,128)}), s32[8,1,512]{2,1,0:T(1,128)S(1)}, u32[]{:S(2)}, u32[]{:S(2)}) async-start(s32[8,1,512]{2,1,0:T(1,128)} %copy.19), calls=%async_computation.1 | async-start | bytes 32768 | tf_op jit(solution)/shard_map/all_to_all | solution.py:83
  45.9 15.3 %all-to-all-start.7 = ((s32[16,1,512]{2,1,0:T(1,128)}), s32[16,1,512]{2,1,0:T(1,128)S(1)}, u32[]{:S(2)}, u32[]{:S(2)}) async-start(s32[16,1,512]{2,1,0:T(1,128)} %copy.23), calls=%async_computation.7 | async-start | bytes 65536 | tf_op jit(solution)/shard_map/all_to_all | solution.py:98
  61.2 5.6 copy-start.1
  61.2 5.6 copy-start.2
  61.2 106.4 %copy-start = (s32[2048]{0:T(1024)S(1)}, s32[2048]{0:T(1024)}, u32[]{:S(2)}) copy-start(s32[2048]{0:T(1024)} %param.10) | copy-start | bytes 24580
  61.2 99.5 %all-to-all-start.3 = ((bf16[8,512,1024]{2,1,0:T(8,128)(2,1)}), bf16[8,512,1024]{2,1,0:T(8,128)(2,1)}, u32[]{:S(2)}, u32[]{:S(2)}) async-start(bf16[8,512,1024]{2,1,0:T(8,128)(2,1)} %gather_fusion.2), calls=%async_computation.3 | async-start | bytes 16777216 | tf_op jit(solution)/shard_map/all_to_all | solution.py:81
  160.7 50.3 %all-to-all-start.6 = ((s32[16,1,512]{2,1,0:T(1,128)}), s32[16,1,512]{2,1,0:T(1,128)S(1)}, u32[]{:S(2)}, u32[]{:S(2)}) async-start(s32[16,1,512]{2,1,0:T(1,128)} %copy.22), calls=%async_computation.6 | async-start | bytes 65536 | tf_op jit(solution)/shard_map/all_to_all | solution.py:99
  211.0 13.6 %all-to-all-start.4 = ((f32[8,1,512]{2,1,0:T(1,128)}), f32[8,1,512]{2,1,0:T(1,128)S(1)}, u32[]{:S(2)}, u32[]{:S(2)}) async-start(f32[8,1,512]{2,1,0:T(1,128)} %all_to_all.76), calls=%async_computation.4 | async-start | bytes 32768 | tf_op jit(solution)/shard_map/all_to_all | solution.py:88
  224.6 259.1 %all-to-all-start.8 = ((bf16[16,512,1024]{2,1,0:T(8,128)(2,1)}), bf16[16,512,1024]{2,1,0:T(8,128)(2,1)}, u32[]{:S(2)}, u32[]{:S(2)}) async-start(bf16[16,512,1024]{2,1,0:T(8,128)(2,1)} %gather_fusion.5), calls=%async_computation.8 | async-start | bytes 33554432 | tf_op jit(solution)/shard_map/all_to_all | solution.py:97
where the time goes:
time: 583 us; the launch traced here: 580 us
  waiting for transfers between devices  356 us (61%)
  matrix products  59.5 us (10%)
  local copies, waits for them, and re-layouts  59.4 us (10%)
  starting transfers between devices  51.2 us (9%)
  loops' own time  30.9 us (5%)
  other arithmetic  14.1 us (2%)
  blocking collectives  9 us (2%)
    all_to_all x1, waiting for transfers between devices, on_device(): lax.all_to_all(piece_rows[grp_asked], 'grp', split_axis=0, concat_axis=0,...  252 us
    all_to_all x1, waiting for transfers between devices, on_device(): lax.all_to_all(piece_rows[asked], 'clus', split_axis=0, concat_axis=0, ti...  92.6 us
    dot_general x24, matrix products, score_pair(): cosine = jnp.dot(own_rows, part_rows.T, preferred_element_type=jnp.float32)  59.5 us
    another operation x2, loops' own time, local_pairs(): lax.scan(visit, best_sim, (arrived[0], arrived[1], arrived[2], own_picks,...  30.9 us
    dynamic_slice x72, local copies, waits for them, and re-layouts, local_pairs(): lax.scan(visit, best_sim, (arrived[0], arrived[1], arrived[2], own_picks,...  29.2 us
  transfers between devices with their start and end apart: 9, of which 5 were waited for; matrix products, arithmetic and copies ran while one was open for 11% of the time, Pallas kernels for 0%

commit v1 on v0

v1 whole, which is shorter than its diff:
```python
import jax
import jax.numpy as jnp
from jax import lax
from jax.experimental import pallas as pl
from jax.experimental.pallas import tpu as pltpu
from jax.sharding import PartitionSpec as P

MESH = pl.DeviceIdType.MESH
ROWS = 2048
D = 1024
BLOCK = 512
BLOCKS = ROWS // BLOCK
EPS = 1e-06
FILL = -1.0

PIECE = 256
PIECES = ROWS // PIECE
CHUNK = 128
CHUNKS = ROWS // CHUNK
PER = PIECE // CHUNK

EE_HUB = [(0, 0, 0), (0, 0, 2), (0, 1, 0), (0, 1, 1), (0, 2, 0), (0, 3, 0), (2, 3, 0), (1, 2, 0), (1, 2, 1),
          (1, 3, 0), (1, 3, 1), (0, 4, 0), (0, 4, 1), (1, 4, 0), (1, 4, 1), (3, 4, 0), (3, 4, 1)]
EL_HUB = [(1, 0, 0), (1, 1, 0), (2, 1, 0), (2, 1, 1), (3, 2, 0), (3, 2, 1), (4, 1, 0), (4, 1, 1),
          (0, 2, 0), (0, 2, 1), (1, 2, 0), (1, 2, 1)]
LL_HUB = [(0, 1, 0), (1, 2, 0), (1, 2, 1)]
EE_CLUS = [(0, 0, 0), (0, 0, 2), (0, 1, 0), (0, 1, 1)]
EL_CLUS = [(0, 2, 0), (0, 2, 1), (0, 3, 0), (0, 3, 1), (1, 2, 0), (1, 2, 1), (1, 3, 0), (1, 3, 1)]
LL_CLUS = [(0, 2, 0), (0, 3, 0), (1, 2, 0), (1, 3, 0)]
PLACE_A = [(0, 0), (0, 3), (3, 0), (1, 0), (3, 1), (3, 3), (1, 3), (3, 2), (0, 0)]
PLACE_B = [(0, 0), (0, 1), (3, 0), (1, 0), (0, 3), (3, 1), (1, 1), (0, 2), (0, 0)]
PLACE_C = [(0, 0), (0, 1), (0, 0), (0, 0), (0, 0), (3, 1), (3, 0), (1, 1), (1, 0)]
LATE = 5
WORD = 9


def packed(values, bits):
    words = [0, 0]
    for at, value in enumerate(values):
        words[at // WORD] |= value << bits * (at % WORD)
    return words


def flags(values):
    return sum(int(value) << at for at, value in enumerate(values))


def kernel(emb, labs, own_tab, part_tab, live_tab, out, early, late, meta_e, meta_l, tabs, best, ret,
           in_sem, tab_sem, own_send, fwd_send, meta_send, ret_send,
           e1_recv, e2_recv, l0_recv, one_recv, x_recv, meta_recv, ret_recv):
    c = lax.axis_index("clus")
    g = lax.axis_index("grp")
    x, k = c // 2, c % 2
    z, y = g // 4, g % 4
    yy = (y + 2 * k) % 4
    hub = yy < 2
    hub_f = 1 - yy // 2
    is_a, is_b = yy == 0, yy == 1
    kc = 1 - y // 2

    def dev(dx, core, dz, dy):
        return (((x + dx) % 4) * 2 + core, ((z + dz) % 4) * 4 + (y + dy) % 4)

    up, down = dev(0, k, 1, 0), dev(0, k, 3, 0)
    mate = dev(0, 1 - k, 0, 0)
    x_up, x_down = dev(1, kc, 0, 0), dev(3, kc, 0, 0)
    beside = dev(0, k, 0, 1 + 2 * ((yy + 1) // 2 % 2))

    barrier = pltpu.get_barrier_semaphore()

    def greet(device):
        pl.semaphore_signal(barrier, inc=1, device_id=device, device_id_type=MESH)

    for device in (x_up, x_down, mate):
        greet(device)

    @pl.when(is_a)
    def _():
        for dz, dy in ((1, 0), (3, 0), (0, 1), (3, 1), (0, 3), (1, 3), (3, 3), (3, 2)):
            greet(dev(0, k, dz, dy))

    @pl.when(is_b)
    def _():
        for dz, dy in ((1, 0), (3, 0), (0, 3), (1, 3), (0, 1), (1, 1), (3, 1), (0, 2)):
            greet(dev(0, k, dz, dy))

    @pl.when(yy == 3)
    def _():
        for dz, dy in ((0, 1), (1, 1), (3, 1), (0, 2)):
            greet(dev(0, k, dz, dy))

    @pl.when(yy == 2)
    def _():
        for dz, dy in ((0, 3), (1, 3), (3, 3), (1, 2)):
            greet(dev(0, k, dz, dy))

    @pl.when(hub_f == 0)
    def _():
        for dx in (1, 3):
            greet(dev(dx, 1 - k, 0, 0))

    def part_of(ref, item, at, size):
        per = BLOCK // size
        return ref.at[item, at // per, pl.ds(pl.multiple_of(at % per * size, size), size)]

    def piece_of(ref, item, p):
        return part_of(ref, item, p, PIECE)

    def chunk_of(ref, item, chunk):
        return part_of(ref, item, chunk, CHUNK)

    def piece_in(p):
        return pltpu.make_async_copy(emb.at[pl.ds(p * PIECE, PIECE)], piece_of(early, 0, p), in_sem.at[p])

    for p in range(PIECES):
        piece_in(p).start()
    for b in range(BLOCKS):
        meta_e[0, b, 0:4, :] = labs[4 * b:4 * b + 4, :]
    for at, tab in enumerate((own_tab, part_tab, live_tab)):
        meta_e[0, BLOCKS, at:at + 1, 0:24] = tab[...]

    def remote(src, dst, send, recv, device):
        return pltpu.make_async_remote_copy(src_ref=src, dst_ref=dst, send_sem=send, recv_sem=recv,
                                            device_id=device, device_id_type=MESH)

    def arrived(ref, sem):
        pltpu.make_async_copy(ref, ref, sem).wait()

    def meta_copy(src, dst, item, send, device):
        return remote(src, dst, meta_send.at[send], meta_recv.at[item], device)

    def normalize(p):
        piece_in(p).wait()
        rows = piece_of(early, 0, p)
        wide = rows[...].astype(jnp.float32)
        inverse = lax.rsqrt(jnp.sum(wide * wide, axis=1, keepdims=True) + EPS)
        rows[...] = (wide * inverse).astype(jnp.bfloat16)

    normalize(0)
    pl.semaphore_wait(barrier, 9 + 2 * hub_f)

    x_from = 1 - hub_f
    meta_copy(meta_e.at[0], meta_l.at[x_from], LATE + x_from, 0, x_up).start()
    meta_copy(meta_e.at[0], meta_l.at[2 + x_from], LATE + 2 + x_from, 1, x_down).start()

    @pl.when(hub)
    def _():
        meta_copy(meta_e.at[0], meta_e.at[2], 2, 2, up).start()
        meta_copy(meta_e.at[0], meta_e.at[3], 3, 3, down).start()
        meta_copy(meta_e.at[0], meta_e.at[1], 1, 4, mate).start()

        @pl.when(is_a)
        def _():
            meta_copy(meta_e.at[0], meta_e.at[4], 4, 5, beside).start()

    @pl.when(hub_f == 0)
    def _():
        meta_copy(meta_e.at[0], meta_e.at[1], 1, 2, beside).start()

    def send_own(p):
        piece = piece_of(early, 0, p)
        remote(piece, piece_of(late, x_from, p), own_send.at[0], x_recv.at[x_from], x_up).start()
        remote(piece, piece_of(late, 2 + x_from, p), own_send.at[1], x_recv.at[2 + x_from], x_down).start()

        def part(q, carry):
            chunk = p * PER + q
            src = chunk_of(early, 0, chunk)

            @pl.when(hub)
            def _():
                remote(src, chunk_of(early, 2, chunk), own_send.at[2], e2_recv.at[chunk], up).start()
                remote(src, chunk_of(early, 3, chunk), own_send.at[3], one_recv.at[0], down).start()

                @pl.when(is_a)
                def _():
                    remote(src, chunk_of(early, 4, chunk), own_send.at[4], one_recv.at[1], beside).start()

            @pl.when(hub_f == 0)
            def _():
                remote(src, chunk_of(early, 1, chunk), own_send.at[2], e1_recv.at[chunk], beside).start()
            return carry

        lax.fori_loop(0, PER, part, 0)

        @pl.when(hub)
        def _():
            remote(piece, piece_of(early, 1, p), own_send.at[5], one_recv.at[4], mate).start()

    send_own(0)

    def rest(p, carry):
        normalize(p)
        send_own(p)
        return carry

    lax.fori_loop(1, PIECES, rest, 0)

    @pl.when(hub)
    def _():
        arrived(meta_e.at[1], meta_recv.at[1])
        meta_copy(meta_e.at[1], meta_l.at[0], LATE, 6, up).start()
        meta_copy(meta_e.at[1], meta_l.at[1], LATE + 1, 7, down).start()

        @pl.when(is_a)
        def _():
            meta_copy(meta_e.at[1], meta_l.at[2], LATE + 2, 8, beside).start()

        arrived(meta_e.at[2], meta_recv.at[2])

        @pl.when(is_b)
        def _():
            meta_copy(meta_e.at[2], meta_e.at[4], 4, 5, beside).start()

        def take(chunk, carry):
            src = chunk_of(early, 1, chunk)
            arrived(src, e1_recv.at[chunk])
            remote(src, chunk_of(late, 0, chunk), fwd_send.at[0], l0_recv.at[chunk], up).start()
            remote(src, chunk_of(late, 1, chunk), fwd_send.at[1], one_recv.at[2], down).start()

            @pl.when(is_a)
            def _():
                remote(src, chunk_of(late, 2, chunk), fwd_send.at[2], one_recv.at[3], beside).start()

            arrived(chunk_of(early, 2, chunk), e2_recv.at[chunk])

            @pl.when(is_b)
            def _():
                remote(chunk_of(early, 2, chunk), chunk_of(early, 4, chunk), own_send.at[4], one_recv.at[1], beside).start()
            return carry

        lax.fori_loop(0, CHUNKS, take, 0)
        arrived(meta_l.at[0], meta_recv.at[LATE])

        @pl.when(is_b)
        def _():
            meta_copy(meta_l.at[0], meta_l.at[2], LATE + 2, 8, beside).start()

        arrived(early.at[3], one_recv.at[0])
        arrived(early.at[4], one_recv.at[1])
        for item in (3, 4):
            arrived(meta_e.at[item], meta_recv.at[item])
        for item in (1, 2):
            arrived(meta_l.at[item], meta_recv.at[LATE + item])

    @pl.when(hub_f == 0)
    def _():
        arrived(early.at[1], one_recv.at[4])
        arrived(meta_e.at[1], meta_recv.at[1])
        for item in range(4):
            arrived(meta_l.at[item], meta_recv.at[LATE + item])

    copies = [pltpu.make_async_copy(meta_e.at[item, BLOCKS], tabs.at[item], tab_sem.at[item]) for item in range(5)]
    copies += [pltpu.make_async_copy(meta_l.at[item, BLOCKS], tabs.at[LATE + item], tab_sem.at[LATE + item])
               for item in range(4)]
    for copy in copies:
        copy.start()
    for copy in copies:
        copy.wait()

    best[...] = jnp.full(best.shape, FILL, jnp.float32)

    def by_role(for_hub, for_clus):
        return for_clus + (for_hub - for_clus) * hub_f

    def lists(for_hub, for_clus):
        fields = []
        for f in range(2):
            ours, theirs = packed([e[f] for e in for_hub], 3), packed([e[f] for e in for_clus], 3)
            fields.append([by_role(ours[w], theirs[w]) for w in range(2)])
        return fields + [by_role(flags([e[2] == 1 for e in for_hub]), flags([e[2] == 1 for e in for_clus]))]

    todo = (lists(EE_HUB, EE_CLUS), lists(EL_HUB, EL_CLUS), lists(LL_HUB, LL_CLUS))
    offsets = []
    for f in range(2):
        a, b, c_ = (packed([p[f] for p in place], 2)[0] for place in (PLACE_A, PLACE_B, PLACE_C))
        offsets.append(by_role(a + (b - a) * (yy % 2), c_))

    item_at = lax.broadcasted_iota(jnp.int32, best.shape, 0)
    block_at = lax.broadcasted_iota(jnp.int32, best.shape, 1) // 4

    def pair(kind, at):
        second_word = at // WORD
        shift = 3 * (at - WORD * second_word)
        row, col = (((words[0] + (words[1] - words[0]) * second_word) >> shift) & 7 for words in todo[kind][:2])
        asks = (todo[kind][2] >> at) & 1
        row_item = row + (LATE if kind == 2 else 0)
        col_item = col + (LATE if kind > 0 else 0)
        asker = row_item + (col_item - row_item) * asks
        other = row_item + col_item - asker
        first, second = ((offset >> (2 * other)) & 3 for offset in offsets)
        row_ref, row_meta = (late, meta_l) if kind == 2 else (early, meta_e)
        col_ref, col_meta = (late, meta_l) if kind > 0 else (early, meta_e)
        place_c = ((x + first) % 4) * 2 + (k + second) % 2
        place_g = 8 + ((z + first) % 4) * 4 + (y + second) % 4
        in_grp = hub_f
        if kind == 0:
            own_pair = 1 - jnp.minimum(at // 2, 1)
            in_grp = own_pair * at + (1 - own_pair) * hub_f
        place = in_grp * place_g + (1 - in_grp) * place_c
        row_block = tabs[asker, asks, place]
        col_block = tabs[asker, 1 - asks, place]
        alive = tabs[asker, 2, place]
        rows = row_ref[row, row_block]
        row_labs = [row_meta[row, row_block, i:i + 1, :].astype(jnp.float32) for i in range(4)]
        col_labs = [col_meta[col, col_block, i:i + 1, :].astype(jnp.float32) for i in range(4)]
        row_labs = [jnp.transpose(jnp.broadcast_to(lab, (128, 128))) for lab in row_labs]
        row_best = [None] * 4
        col_best = [None] * 4
        if kind == 0:
            apart = jnp.where((row == col) & (row_block == col_block), 0, 1)
            off = (lax.broadcasted_iota(jnp.int32, (128, 128), 0) != lax.broadcasted_iota(jnp.int32, (128, 128), 1))
            off = off | (jnp.full((128, 128), apart, jnp.int32) > 0)
        half = BLOCK // 2
        for n in range(2):
            cols = col_ref[col, col_block, n * half:(n + 1) * half, :]
            cosine = lax.dot_general(rows, cols, (((1,), (1,)), ((), ())), preferred_element_type=jnp.float32)
            for jj in range(2):
                j = 2 * n + jj
                for i in range(4):
                    tile = cosine[i * 128:(i + 1) * 128, jj * 128:(jj + 1) * 128]
                    keep = row_labs[i] == col_labs[j]
                    if kind == 0 and i == j:
                        keep = keep & off
                    tile = jnp.where(keep, tile, FILL)
                    row_best[i] = tile if row_best[i] is None else jnp.maximum(row_best[i], tile)
                    folded = jnp.max(tile.reshape(16, 8, 128), axis=0)
                    col_best[j] = folded if col_best[j] is None else jnp.maximum(col_best[j], folded)
        row_best = jnp.concatenate([jnp.max(jnp.transpose(t), axis=0, keepdims=True) for t in row_best] * 4, axis=0)
        col_best = jnp.concatenate([jnp.max(t, axis=0, keepdims=True) for t in col_best] * 4, axis=0)
        now = best[...]
        for values, item, block in ((row_best, row_item, row_block), (col_best, col_item, col_block)):
            hit = (item_at == item) & (block_at == block) & (jnp.full(best.shape, alive, jnp.int32) > 0)
            now = jnp.maximum(now, jnp.where(hit, values[None], FILL))
        best[...] = now

    def first_step(at, carry):
        @pl.when(hub & (at < CHUNKS))
        def _():
            src = chunk_of(late, 0, at)
            arrived(src, l0_recv.at[at])

            @pl.when(is_b)
            def _():
                remote(src, chunk_of(late, 2, at), fwd_send.at[2], one_recv.at[3], beside).start()
        pair(0, at)
        return carry

    lax.fori_loop(0, len(EE_CLUS) + (len(EE_HUB) - len(EE_CLUS)) * hub_f, first_step, 0)

    @pl.when(hub)
    def _():
        arrived(late.at[1], one_recv.at[2])
        arrived(late.at[2], one_recv.at[3])

    @pl.when(hub_f == 0)
    def _():
        for item in range(4):
            arrived(late.at[item], x_recv.at[item])

    def second_step(at, carry):
        pair(1, at)
        return carry

    def third_step(at, carry):
        pair(2, at)
        return carry

    lax.fori_loop(0, len(EL_CLUS) + (len(EL_HUB) - len(EL_CLUS)) * hub_f, second_step, 0)
    lax.fori_loop(0, len(LL_CLUS) + (len(LL_HUB) - len(LL_CLUS)) * hub_f, third_step, 0)

    def give(item, to, send, device):
        return remote(best.at[item], ret.at[to], ret_send.at[send], ret_recv.at[to], device)

    def hub_gives(a):
        return [give(1, 0, 0, dev(0, k, 0, 3 if a else 1)), give(2, 0, 1, dev(0, k, 3, 0)), give(3, 1, 2, dev(0, k, 1, 0)),
                give(4, 2, 3, dev(0, k, 3, 1) if a else dev(0, k, 0, 3)),
                give(5, 1, 4, dev(0, k, 3, 3 if a else 1)), give(6, 2, 5, dev(0, k, 1, 3 if a else 1)),
                give(7, 3, 6, dev(0, k, 3, 2) if a else dev(0, k, 0, 2))]

    def clus_gives():
        return [give(1, 3, 0, mate), give(5, 4, 1, dev(3, 1 - k, 0, 0)), give(6, 4, 2, dev(3, k, 0, 0)),
                give(7, 5, 3, dev(1, 1 - k, 0, 0)), give(8, 5, 4, dev(1, k, 0, 0))]

    for which, gives in ((is_a, lambda: hub_gives(True)), (is_b, lambda: hub_gives(False)), (hub_f == 0, clus_gives)):
        @pl.when(which)
        def _(gives=gives):
            for copy in gives():
                copy.start()

    for s in range(2):
        arrived(early.at[0], own_send.at[s])
        arrived(meta_e.at[0], meta_send.at[s])

    @pl.when(hub)
    def _():
        for s in range(2, 6):
            arrived(early.at[0], own_send.at[s])
        for s in range(3):
            arrived(early.at[0], fwd_send.at[s])
        for s in range(2, 9):
            arrived(meta_e.at[0], meta_send.at[s])
        for s in range(7):
            arrived(best.at[0], ret_send.at[s])

    @pl.when(hub_f == 0)
    def _():
        arrived(early.at[0], own_send.at[2])
        arrived(meta_e.at[0], meta_send.at[2])
        for s in range(5):
            arrived(best.at[0], ret_send.at[s])

    result = best[0]
    for j in range(6):
        arrived(ret.at[j], ret_recv.at[j])
        result = jnp.maximum(result, ret[j])
    out[...] = result


def on_device(embeddings, labels, partner_block, own_block, live):
    dma = pltpu.SemaphoreType.DMA
    vmem = pl.BlockSpec(memory_space=pltpu.VMEM)
    best = pl.pallas_call(
        kernel,
        out_shape=jax.ShapeDtypeStruct((16, 128), jnp.float32),
        in_specs=[pl.BlockSpec(memory_space=pl.ANY), vmem, vmem, vmem, vmem],
        out_specs=vmem,
        scratch_shapes=[
            pltpu.VMEM((5, BLOCKS, BLOCK, D), jnp.bfloat16),
            pltpu.VMEM((4, BLOCKS, BLOCK, D), jnp.bfloat16),
            pltpu.VMEM((5, BLOCKS + 1, 8, 128), jnp.int32),
            pltpu.VMEM((4, BLOCKS + 1, 8, 128), jnp.int32),
            pltpu.SMEM((9, 8, 128), jnp.int32),
            pltpu.VMEM((9, 16, 128), jnp.float32),
            pltpu.VMEM((6, 16, 128), jnp.float32),
            dma((PIECES,)), dma((9,)), dma((6,)), dma((3,)), dma((9,)), dma((7,)),
            dma((CHUNKS,)), dma((CHUNKS,)), dma((CHUNKS,)), dma((5,)), dma((4,)), dma((9,)), dma((6,)),
        ],
        compiler_params=pltpu.CompilerParams(collective_id=0, has_side_effects=True, vmem_limit_bytes=56 << 20),
        cost_estimate=pl.CostEstimate(flops=24 * 2 * 512 * 512 * 1024, bytes_accessed=4 << 20, transcendentals=2048),
    )(embeddings, labels.reshape(16, 128), own_block, partner_block, live)
    return best.reshape(2048)


def solution(mesh):
    placed = (
        P(("clus", "grp"), None),
        P(("clus", "grp")),
        P(("clus", "grp"), None),
        P(("clus", "grp"), None),
        P(("clus", "grp"), None),
    )
    return jax.shard_map(
        on_device, mesh=mesh, in_specs=placed, out_specs=P(("clus", "grp")), check_vma=False
    )
```

time: 583 us -> 125 us (0.21)
  waiting for transfers between devices: 356 us -> 0 us
  Pallas kernels: 0 us -> 122 us
  matrix products: 59.5 us -> 0 us
  local copies, waits for them, and re-layouts: 59.4 us -> 1.3 us
  starting transfers between devices: 51.2 us -> 0 us
  loops' own time: 30.9 us -> 0 us
  other arithmetic: 14.1 us -> 0 us
  blocking collectives: 9 us -> 0 us
    all_to_all x9 -> x0, waiting for transfers between devices: 356 us -> none  [the longest x1 252 us: on_device(): lax.all_to_all(piece_rows[grp_asked], 'grp', split_axis=0, concat_axis=0,...]
    pallas_call x0 -> x1, Pallas kernels: none -> 122 us  [on_device(): pl.pallas_call(kernel, out_shape=jax.ShapeDtypeStruct((16, 128), jnp.floa...]
    dot_general x24 -> x0, matrix products: 59.5 us -> none  [score_pair(): cosine = jnp.dot(own_rows, part_rows.T, preferred_element_type=jnp.float32)]
    all_to_all x9 -> x0, starting transfers between devices: 51.2 us -> none  [the longest x1 7.77 us: on_device(): lax.all_to_all(grp_wanted.reshape(grp_count, 1), 'grp', split_axis=0, con...]
    dynamic_slice x120 -> x0, local copies, waits for them, and re-layouts: 32.9 us -> none  [the longest x72 29.2 us: local_pairs(): lax.scan(visit, best_sim, (arrived[0], arrived[1], arrived[2], own_picks,...]
    another operation x2 -> x0, loops' own time: 30.9 us -> none  [local_pairs(): lax.scan(visit, best_sim, (arrived[0], arrived[1], arrived[2], own_picks,...]
    gather x6 -> x0, local copies, waits for them, and re-layouts: 18.3 us -> none  [the longest x1 9.22 us: on_device(): piece_rows[grp_asked]]
    all_to_all x1 -> x0, blocking collectives: 9 us -> none  [on_device(): lax.all_to_all(grp_cols, 'grp', split_axis=0, concat_axis=0, tiled=True)]
  transfers between devices with their start and end apart: 9 -> 0, of which waited for: 5 -> 0; matrix products, arithmetic and copies ran while one was open for 11% -> 0% of each run, Pallas kernels for 0% -> 0%
where the time goes in v1:
time: 125 us; the launch traced here: 124 us
  Pallas kernels  122 us (98%)
  local copies, waits for them, and re-layouts  1.3 us (1%)
    pallas_call x1, Pallas kernels, on_device(): pl.pallas_call(kernel, out_shape=jax.ShapeDtypeStruct((16, 128), jnp.floa...  122 us

profile of v1, /device:TPU:1, one launch (start us, length us, event | category | flops | bytes accessed | tf_op | source)
XLA Modules:
  0.0 123.5 jit_solution(7014703774454736100)
XLA Ops:
  0.0 122.2 %shard_map.55 = f32[16,128]{1,0:T(8,128)} custom-call(bf16[2048,1024]{1,0:T(8,128)(2,1)} %emb.1, s32[16,128]{1,0:T(8,128)} %bitcast.3, s32[1,24]{1,0:T(1,128)} %own_tab.1, s32[1,24]{1,0:T(1,128)} %part_tab.1, s32[1,24]{1,0:T(1,128)} %live_tab.1), custom_call_target="tpu_custom_call" | custom-call | flops 12884901888 | bytes 4194304 | tf_op jit(solution)/shard_map/pallas_call | solution.py:422
  122.2 1.3 %copy.7 = f32[2048]{0:T(1024)} copy(f32[2048]{0:T(1024)} %bitcast.2) | data formatting | bytes 16384

commit v2 on v1

--- a/solution.py
+++ b/solution.py
@@ -19,13 +19,14 @@
 CHUNKS = ROWS // CHUNK
 PER = PIECE // CHUNK
 
-EE_HUB = [(0, 0, 0), (0, 0, 2), (0, 1, 0), (0, 1, 1), (0, 2, 0), (0, 3, 0), (2, 3, 0), (1, 2, 0), (1, 2, 1),
-          (1, 3, 0), (1, 3, 1), (0, 4, 0), (0, 4, 1), (1, 4, 0), (1, 4, 1), (3, 4, 0), (3, 4, 1)]
-EL_HUB = [(1, 0, 0), (1, 1, 0), (2, 1, 0), (2, 1, 1), (3, 2, 0), (3, 2, 1), (4, 1, 0), (4, 1, 1),
+EE_HUB = [(0, 0, 0), (0, 0, 0), (0, 1, 0), (0, 1, 1), (0, 2, 0), (0, 3, 0), (2, 3, 0), (1, 2, 0), (1, 2, 1),
+          (1, 3, 0), (1, 3, 1), (0, 4, 0), (0, 4, 1), (1, 4, 0), (1, 4, 1), (3, 4, 0), (3, 4, 1), (3, 4, 1)]
+EL_HUB = [(1, 0, 0), (1, 1, 0), (2, 1, 0), (2, 1, 1), (4, 1, 0), (4, 1, 1), (3, 2, 0), (3, 2, 1),
           (0, 2, 0), (0, 2, 1), (1, 2, 0), (1, 2, 1)]
-LL_HUB = [(0, 1, 0), (1, 2, 0), (1, 2, 1)]
-EE_CLUS = [(0, 0, 0), (0, 0, 2), (0, 1, 0), (0, 1, 1)]
-EL_CLUS = [(0, 2, 0), (0, 2, 1), (0, 3, 0), (0, 3, 1), (1, 2, 0), (1, 2, 1), (1, 3, 0), (1, 3, 1)]
+LL_HUB = [(0, 1, 0), (1, 2, 0), (1, 2, 1), (1, 2, 1)]
+EE_CLUS = [(0, 0, 0), (0, 0, 0), (0, 1, 0), (0, 1, 1)]
+EL_CLUS = [(0, 2, 0), (0, 2, 1), (1, 2, 0), (1, 2, 1), (0, 3, 0), (0, 3, 1), (1, 3, 0), (1, 3, 1),
+           (0, 2, 0), (0, 2, 1), (1, 2, 0), (1, 2, 1)]
 LL_CLUS = [(0, 2, 0), (0, 3, 0), (1, 2, 0), (1, 3, 0)]
 PLACE_A = [(0, 0), (0, 3), (3, 0), (1, 0), (3, 1), (3, 3), (1, 3), (3, 2), (0, 0)]
 PLACE_B = [(0, 0), (0, 1), (3, 0), (1, 0), (0, 3), (3, 1), (1, 1), (0, 2), (0, 0)]
@@ -47,7 +48,7 @@
 
 def kernel(emb, labs, own_tab, part_tab, live_tab, out, early, late, meta_e, meta_l, tabs, best, ret,
            in_sem, tab_sem, own_send, fwd_send, meta_send, ret_send,
-           e1_recv, e2_recv, l0_recv, one_recv, x_recv, meta_recv, ret_recv):
+           e1_recv, e2_recv, late_recv, one_recv, meta_recv, ret_recv):
     c = lax.axis_index("clus")
     g = lax.axis_index("grp")
     x, k = c // 2, c % 2
@@ -68,36 +69,17 @@
 
     barrier = pltpu.get_barrier_semaphore()
 
-    def greet(device):
-        pl.semaphore_signal(barrier, inc=1, device_id=device, device_id_type=MESH)
-
-    for device in (x_up, x_down, mate):
-        greet(device)
-
-    @pl.when(is_a)
-    def _():
-        for dz, dy in ((1, 0), (3, 0), (0, 1), (3, 1), (0, 3), (1, 3), (3, 3), (3, 2)):
-            greet(dev(0, k, dz, dy))
-
-    @pl.when(is_b)
-    def _():
-        for dz, dy in ((1, 0), (3, 0), (0, 3), (1, 3), (0, 1), (1, 1), (3, 1), (0, 2)):
-            greet(dev(0, k, dz, dy))
-
-    @pl.when(yy == 3)
-    def _():
-        for dz, dy in ((0, 1), (1, 1), (3, 1), (0, 2)):
-            greet(dev(0, k, dz, dy))
-
-    @pl.when(yy == 2)
-    def _():
-        for dz, dy in ((0, 3), (1, 3), (3, 3), (1, 2)):
-            greet(dev(0, k, dz, dy))
+    def greet(*devices):
+        for device in devices:
+            pl.semaphore_signal(barrier, inc=1, device_id=device, device_id_type=MESH)
+
+    @pl.when(hub)
+    def _():
+        greet(up, down, beside, dev(0, k, 0, 3 - 2 * (yy % 2)))
 
     @pl.when(hub_f == 0)
     def _():
-        for dx in (1, 3):
-            greet(dev(dx, 1 - k, 0, 0))
+        greet(mate, x_up, x_down, dev(1, 1 - k, 0, 0), dev(3, 1 - k, 0, 0))
 
     def part_of(ref, item, at, size):
         per = BLOCK // size
@@ -137,7 +119,7 @@
         rows[...] = (wide * inverse).astype(jnp.bfloat16)
 
     normalize(0)
-    pl.semaphore_wait(barrier, 9 + 2 * hub_f)
+    pl.semaphore_wait(barrier, 3 + 3 * hub_f)
 
     x_from = 1 - hub_f
     meta_copy(meta_e.at[0], meta_l.at[x_from], LATE + x_from, 0, x_up).start()
@@ -159,8 +141,8 @@
 
     def send_own(p):
         piece = piece_of(early, 0, p)
-        remote(piece, piece_of(late, x_from, p), own_send.at[0], x_recv.at[x_from], x_up).start()
-        remote(piece, piece_of(late, 2 + x_from, p), own_send.at[1], x_recv.at[2 + x_from], x_down).start()
+        remote(piece, piece_of(late, x_from, p), own_send.at[0], late_recv.at[x_from, p], x_up).start()
+        remote(piece, piece_of(late, 2 + x_from, p), own_send.at[1], late_recv.at[2 + x_from, p], x_down).start()
 
         def part(q, carry):
             chunk = p * PER + q
@@ -184,7 +166,7 @@
 
         @pl.when(hub)
         def _():
-            remote(piece, piece_of(early, 1, p), own_send.at[5], one_recv.at[4], mate).start()
+            remote(piece, piece_of(early, 1, p), own_send.at[5], one_recv.at[2], mate).start()
 
     send_own(0)
 
@@ -214,12 +196,12 @@
         def take(chunk, carry):
             src = chunk_of(early, 1, chunk)
             arrived(src, e1_recv.at[chunk])
-            remote(src, chunk_of(late, 0, chunk), fwd_send.at[0], l0_recv.at[chunk], up).start()
-            remote(src, chunk_of(late, 1, chunk), fwd_send.at[1], one_recv.at[2], down).start()
+            remote(src, chunk_of(late, 0, chunk), fwd_send.at[0], late_recv.at[0, chunk], up).start()
+            remote(src, chunk_of(late, 1, chunk), fwd_send.at[1], late_recv.at[1, chunk], down).start()
 
             @pl.when(is_a)
             def _():
-                remote(src, chunk_of(late, 2, chunk), fwd_send.at[2], one_recv.at[3], beside).start()
+                remote(src, chunk_of(late, 2, chunk), fwd_send.at[2], late_recv.at[2, chunk], beside).start()
 
             arrived(chunk_of(early, 2, chunk), e2_recv.at[chunk])
 
@@ -244,7 +226,7 @@
 
     @pl.when(hub_f == 0)
     def _():
-        arrived(early.at[1], one_recv.at[4])
+        arrived(early.at[1], one_recv.at[2])
         arrived(meta_e.at[1], meta_recv.at[1])
         for item in range(4):
             arrived(meta_l.at[item], meta_recv.at[LATE + item])
@@ -275,10 +257,10 @@
         a, b, c_ = (packed([p[f] for p in place], 2)[0] for place in (PLACE_A, PLACE_B, PLACE_C))
         offsets.append(by_role(a + (b - a) * (yy % 2), c_))
 
-    item_at = lax.broadcasted_iota(jnp.int32, best.shape, 0)
-    block_at = lax.broadcasted_iota(jnp.int32, best.shape, 1) // 4
-
-    def pair(kind, at):
+    line = lax.broadcasted_iota(jnp.int32, (16, 128), 0)
+    block_at = line // 4
+
+    def look_up(kind, at):
         second_word = at // WORD
         shift = 3 * (at - WORD * second_word)
         row, col = (((words[0] + (words[1] - words[0]) * second_word) >> shift) & 7 for words in todo[kind][:2])
@@ -288,8 +270,6 @@
         asker = row_item + (col_item - row_item) * asks
         other = row_item + col_item - asker
         first, second = ((offset >> (2 * other)) & 3 for offset in offsets)
-        row_ref, row_meta = (late, meta_l) if kind == 2 else (early, meta_e)
-        col_ref, col_meta = (late, meta_l) if kind > 0 else (early, meta_e)
         place_c = ((x + first) % 4) * 2 + (k + second) % 2
         place_g = 8 + ((z + first) % 4) * 4 + (y + second) % 4
         in_grp = hub_f
@@ -297,76 +277,113 @@
             own_pair = 1 - jnp.minimum(at // 2, 1)
             in_grp = own_pair * at + (1 - own_pair) * hub_f
         place = in_grp * place_g + (1 - in_grp) * place_c
-        row_block = tabs[asker, asks, place]
-        col_block = tabs[asker, 1 - asks, place]
-        alive = tabs[asker, 2, place]
+        return row, col, row_item, col_item, tabs[asker, asks, place], tabs[asker, 1 - asks, place], tabs[asker, 2, place]
+
+    def labels_down(meta, item, block):
+        labs = [meta[item, block, i:i + 1, :].astype(jnp.float32) for i in range(4)]
+        return [jnp.transpose(jnp.broadcast_to(lab, (128, 128))) for lab in labs]
+
+    def raise_best(item, values, where):
+        best[item] = jnp.maximum(best[item], jnp.where(where, values, FILL))
+
+    def full(scalar):
+        return jnp.full((16, 128), scalar, jnp.int32)
+
+    def score(rows, cols, row_labs, col_labs, off, row_best, col_best):
+        cosine = lax.dot_general(rows, cols, (((1,), (1,)), ((), ())), preferred_element_type=jnp.float32)
+        for j, col_lab in enumerate(col_labs):
+            line_best = None
+            for i in range(4):
+                tile = cosine[i * 128:(i + 1) * 128, j * 128:(j + 1) * 128]
+                keep = row_labs[i] == col_lab
+                if off is not None and i == len(col_best):
+                    keep = keep & off
+                tile = jnp.where(keep, tile, FILL)
+                row_best[i] = tile if row_best[i] is None else jnp.maximum(row_best[i], tile)
+                folded = jnp.max(tile.reshape(16, 8, 128), axis=0)
+                line_best = folded if line_best is None else jnp.maximum(line_best, folded)
+            col_best.append(jnp.max(line_best, axis=0, keepdims=True))
+
+    def down_rows(row_best):
+        return jnp.concatenate([jnp.max(jnp.transpose(t), axis=0, keepdims=True) for t in row_best] * 4, axis=0)
+
+    def pair(kind, at):
+        row, col, row_item, col_item, row_block, col_block, alive = look_up(kind, at)
+        row_ref, row_meta = (late, meta_l) if kind == 2 else (early, meta_e)
+        col_ref, col_meta = (late, meta_l) if kind > 0 else (early, meta_e)
         rows = row_ref[row, row_block]
-        row_labs = [row_meta[row, row_block, i:i + 1, :].astype(jnp.float32) for i in range(4)]
+        row_labs = labels_down(row_meta, row, row_block)
         col_labs = [col_meta[col, col_block, i:i + 1, :].astype(jnp.float32) for i in range(4)]
-        row_labs = [jnp.transpose(jnp.broadcast_to(lab, (128, 128))) for lab in row_labs]
-        row_best = [None] * 4
-        col_best = [None] * 4
+        off = None
         if kind == 0:
             apart = jnp.where((row == col) & (row_block == col_block), 0, 1)
             off = (lax.broadcasted_iota(jnp.int32, (128, 128), 0) != lax.broadcasted_iota(jnp.int32, (128, 128), 1))
             off = off | (jnp.full((128, 128), apart, jnp.int32) > 0)
-        half = BLOCK // 2
+        row_best, col_best = [None] * 4, []
         for n in range(2):
-            cols = col_ref[col, col_block, n * half:(n + 1) * half, :]
-            cosine = lax.dot_general(rows, cols, (((1,), (1,)), ((), ())), preferred_element_type=jnp.float32)
-            for jj in range(2):
-                j = 2 * n + jj
-                for i in range(4):
-                    tile = cosine[i * 128:(i + 1) * 128, jj * 128:(jj + 1) * 128]
-                    keep = row_labs[i] == col_labs[j]
-                    if kind == 0 and i == j:
-                        keep = keep & off
-                    tile = jnp.where(keep, tile, FILL)
-                    row_best[i] = tile if row_best[i] is None else jnp.maximum(row_best[i], tile)
-                    folded = jnp.max(tile.reshape(16, 8, 128), axis=0)
-                    col_best[j] = folded if col_best[j] is None else jnp.maximum(col_best[j], folded)
-        row_best = jnp.concatenate([jnp.max(jnp.transpose(t), axis=0, keepdims=True) for t in row_best] * 4, axis=0)
-        col_best = jnp.concatenate([jnp.max(t, axis=0, keepdims=True) for t in col_best] * 4, axis=0)
-        now = best[...]
-        for values, item, block in ((row_best, row_item, row_block), (col_best, col_item, col_block)):
-            hit = (item_at == item) & (block_at == block) & (jnp.full(best.shape, alive, jnp.int32) > 0)
-            now = jnp.maximum(now, jnp.where(hit, values[None], FILL))
-        best[...] = now
-
-    def first_step(at, carry):
-        @pl.when(hub & (at < CHUNKS))
-        def _():
-            src = chunk_of(late, 0, at)
-            arrived(src, l0_recv.at[at])
-
-            @pl.when(is_b)
-            def _():
-                remote(src, chunk_of(late, 2, at), fwd_send.at[2], one_recv.at[3], beside).start()
-        pair(0, at)
+            cols = col_ref[col, col_block, n * PIECE:(n + 1) * PIECE, :]
+            score(rows, cols, row_labs, col_labs[2 * n:2 * n + 2], off, row_best, col_best)
+        raise_best(row_item, down_rows(row_best), (block_at == row_block) & (full(alive) > 0))
+        raise_best(col_item, jnp.concatenate(col_best * 4, axis=0), (block_at == col_block) & (full(alive) > 0))
+
+    def late_pair(at, p):
+        row, col, row_item, col_item, row_block, col_block, alive = look_up(1, at)
+        block, half = p // 2, p % 2
+        rows = early[row, row_block]
+        row_labs = labels_down(meta_e, row, row_block)
+        col_labs = [meta_l[col, block, pl.ds(half * 2 + j, 1), :].astype(jnp.float32) for j in range(2)]
+        row_best, col_best = [None] * 4, []
+        score(rows, piece_of(late, col, p)[...], row_labs, col_labs, None, row_best, col_best)
+        asked = full(jnp.where(col_block == block, alive, 0)) > 0
+        raise_best(row_item, down_rows(row_best), (block_at == row_block) & asked)
+        at_line = block * 4 + half * 2
+        both = jnp.where(line == at_line, col_best[0], col_best[1])
+        raise_best(col_item, both, asked & ((line == at_line) | (line == at_line + 1)))
+
+    def pass_on(chunk):
+        src = chunk_of(late, 0, chunk)
+        arrived(src, late_recv.at[0, chunk])
+
+        @pl.when(is_b)
+        def _():
+            remote(src, chunk_of(late, 2, chunk), fwd_send.at[2], late_recv.at[2, chunk], beside).start()
+
+    early_pairs = len(EE_CLUS) + (len(EE_HUB) - len(EE_CLUS)) * hub_f
+
+    def step(p, carry):
+        @pl.when(hub)
+        def _():
+            pass_on(2 * p)
+
+        @pl.when(2 * p < early_pairs)
+        def _():
+            pair(0, 2 * p)
+            pair(0, 2 * p + 1)
+
+        @pl.when(hub)
+        def _():
+            pass_on(2 * p + 1)
+            for item in (1, 2):
+                for chunk in (2 * p, 2 * p + 1):
+                    arrived(chunk_of(late, item, chunk), late_recv.at[item, chunk])
+
+        @pl.when(hub_f == 0)
+        def _():
+            for item in range(4):
+                arrived(piece_of(late, item, p), late_recv.at[item, p])
+
+        for at in range(len(EL_HUB)):
+            late_pair(at, p)
         return carry
 
-    lax.fori_loop(0, len(EE_CLUS) + (len(EE_HUB) - len(EE_CLUS)) * hub_f, first_step, 0)
-
     @pl.when(hub)
     def _():
-        arrived(late.at[1], one_recv.at[2])
-        arrived(late.at[2], one_recv.at[3])
-
-    @pl.when(hub_f == 0)
-    def _():
-        for item in range(4):
-            arrived(late.at[item], x_recv.at[item])
-
-    def second_step(at, carry):
-        pair(1, at)
-        return carry
-
-    def third_step(at, carry):
+        pair(0, 16)
+        pair(0, 17)
+
+    lax.fori_loop(0, PIECES, step, 0)
+    for at in range(len(LL_HUB)):
         pair(2, at)
-        return carry
-
-    lax.fori_loop(0, len(EL_CLUS) + (len(EL_HUB) - len(EL_CLUS)) * hub_f, second_step, 0)
-    lax.fori_loop(0, len(LL_CLUS) + (len(LL_HUB) - len(LL_CLUS)) * hub_f, third_step, 0)
 
     def give(item, to, send, device):
         return remote(best.at[item], ret.at[to], ret_send.at[send], ret_recv.at[to], device)
@@ -433,7 +450,7 @@
             pltpu.VMEM((9, 16, 128), jnp.float32),
             pltpu.VMEM((6, 16, 128), jnp.float32),
             dma((PIECES,)), dma((9,)), dma((6,)), dma((3,)), dma((9,)), dma((7,)),
-            dma((CHUNKS,)), dma((CHUNKS,)), dma((CHUNKS,)), dma((5,)), dma((4,)), dma((9,)), dma((6,)),
+            dma((CHUNKS,)), dma((CHUNKS,)), dma((4, CHUNKS)), dma((3,)), dma((9,)), dma((6,)),
         ],
         compiler_params=pltpu.CompilerParams(collective_id=0, has_side_effects=True, vmem_limit_bytes=56 << 20),
         cost_estimate=pl.CostEstimate(flops=24 * 2 * 512 * 512 * 1024, bytes_accessed=4 << 20, transcendentals=2048),

time: 125 us -> 118 us (0.944); the launches traced: 124 us -> 118 us
  Pallas kernels: 122 us -> 117 us
    pallas_call x1, Pallas kernels: 122 us -> 117 us  [on_device(): pl.pallas_call(kernel, out_shape=jax.ShapeDtypeStruct((16, 128), jnp.floa...]
where the time goes in v2:
time: 118 us
  Pallas kernels  117 us (99%)
  local copies, waits for them, and re-layouts  1.3 us (1%)
    pallas_call x1, Pallas kernels, on_device(): pl.pallas_call(kernel, out_shape=jax.ShapeDtypeStruct((16, 128), jnp.floa...  117 us

profile of v2, /device:TPU:1, one launch (start us, length us, event | category | flops | bytes accessed | tf_op | source)
XLA Modules:
  0.0 118.3 jit_solution(2711491294370337723)
XLA Ops:
  0.0 117.0 %shard_map.55 = f32[16,128]{1,0:T(8,128)} custom-call(bf16[2048,1024]{1,0:T(8,128)(2,1)} %emb.1, s32[16,128]{1,0:T(8,128)} %bitcast.3, s32[1,24]{1,0:T(1,128)} %own_tab.1, s32[1,24]{1,0:T(1,128)} %part_tab.1, s32[1,24]{1,0:T(1,128)} %live_tab.1), custom_call_target="tpu_custom_call" | custom-call | flops 12884901888 | bytes 4194304 | tf_op jit(solution)/shard_map/pallas_call | solution.py:439
  117.0 1.3 %copy.7 = f32[2048]{0:T(1024)} copy(f32[2048]{0:T(1024)} %bitcast.2) | data formatting | bytes 16384

commit v3 on v2

--- a/solution.py
+++ b/solution.py
@@ -15,7 +15,7 @@
 
 PIECE = 256
 PIECES = ROWS // PIECE
-CHUNK = 128
+CHUNK = 64
 CHUNKS = ROWS // CHUNK
 PER = PIECE // CHUNK
 
@@ -23,11 +23,12 @@
           (1, 3, 0), (1, 3, 1), (0, 4, 0), (0, 4, 1), (1, 4, 0), (1, 4, 1), (3, 4, 0), (3, 4, 1), (3, 4, 1)]
 EL_HUB = [(1, 0, 0), (1, 1, 0), (2, 1, 0), (2, 1, 1), (4, 1, 0), (4, 1, 1), (3, 2, 0), (3, 2, 1),
           (0, 2, 0), (0, 2, 1), (1, 2, 0), (1, 2, 1)]
-LL_HUB = [(0, 1, 0), (1, 2, 0), (1, 2, 1), (1, 2, 1)]
+LL_HUB = [(0, 1, 0), (1, 2, 0), (1, 2, 1), (1, 2, 1), (1, 2, 1)]
 EE_CLUS = [(0, 0, 0), (0, 0, 0), (0, 1, 0), (0, 1, 1)]
-EL_CLUS = [(0, 2, 0), (0, 2, 1), (1, 2, 0), (1, 2, 1), (0, 3, 0), (0, 3, 1), (1, 3, 0), (1, 3, 1),
-           (0, 2, 0), (0, 2, 1), (1, 2, 0), (1, 2, 1)]
-LL_CLUS = [(0, 2, 0), (0, 3, 0), (1, 2, 0), (1, 3, 0)]
+EL_CLUS = [(0, 1, 0), (0, 1, 1), (1, 0, 0), (1, 0, 1), (0, 1, 0), (0, 1, 1),
+           (0, 2, 0), (0, 2, 1), (1, 3, 0), (1, 3, 1), (0, 2, 0), (0, 2, 1)]
+LL_CLUS = [(0, 1, 0), (0, 2, 0), (0, 3, 0), (1, 2, 0), (1, 3, 0)]
+EL_A = 6
 PLACE_A = [(0, 0), (0, 3), (3, 0), (1, 0), (3, 1), (3, 3), (1, 3), (3, 2), (0, 0)]
 PLACE_B = [(0, 0), (0, 1), (3, 0), (1, 0), (0, 3), (3, 1), (1, 1), (0, 2), (0, 0)]
 PLACE_C = [(0, 0), (0, 1), (0, 0), (0, 0), (0, 0), (3, 1), (3, 0), (1, 1), (1, 0)]
@@ -46,9 +47,9 @@
     return sum(int(value) << at for at, value in enumerate(values))
 
 
-def kernel(emb, labs, own_tab, part_tab, live_tab, out, early, late, meta_e, meta_l, tabs, best, ret,
+def kernel(emb, labs, own_tab, part_tab, live_tab, out, early, late_a, late_b, meta_e, meta_l, tabs, best, ret,
            in_sem, tab_sem, own_send, fwd_send, meta_send, ret_send,
-           e1_recv, e2_recv, late_recv, one_recv, meta_recv, ret_recv):
+           e1_recv, e2_recv, l0_recv, late_recv, one_recv, meta_recv, ret_recv):
     c = lax.axis_index("clus")
     g = lax.axis_index("grp")
     x, k = c // 2, c % 2
@@ -141,28 +142,24 @@
 
     def send_own(p):
         piece = piece_of(early, 0, p)
-        remote(piece, piece_of(late, x_from, p), own_send.at[0], late_recv.at[x_from, p], x_up).start()
-        remote(piece, piece_of(late, 2 + x_from, p), own_send.at[1], late_recv.at[2 + x_from, p], x_down).start()
-
-        def part(q, carry):
-            chunk = p * PER + q
-            src = chunk_of(early, 0, chunk)
-
-            @pl.when(hub)
+
+        @pl.when(hub)
+        def _():
+            for q in range(PER):
+                chunk = p * PER + q
+                remote(chunk_of(early, 0, chunk), chunk_of(early, 2, chunk), own_send.at[2], e2_recv.at[chunk], up).start()
+            remote(piece, piece_of(early, 3, p), own_send.at[3], one_recv.at[0], down).start()
+
+            @pl.when(is_a)
             def _():
-                remote(src, chunk_of(early, 2, chunk), own_send.at[2], e2_recv.at[chunk], up).start()
-                remote(src, chunk_of(early, 3, chunk), own_send.at[3], one_recv.at[0], down).start()
-
-                @pl.when(is_a)
-                def _():
-                    remote(src, chunk_of(early, 4, chunk), own_send.at[4], one_recv.at[1], beside).start()
-
-            @pl.when(hub_f == 0)
-            def _():
-                remote(src, chunk_of(early, 1, chunk), own_send.at[2], e1_recv.at[chunk], beside).start()
-            return carry
-
-        lax.fori_loop(0, PER, part, 0)
+                remote(piece, piece_of(early, 4, p), own_send.at[4], one_recv.at[1], beside).start()
+
+        @pl.when(hub_f == 0)
+        def _():
+            remote(piece, piece_of(early, 1, p), own_send.at[2], e1_recv.at[p], beside).start()
+
+        remote(piece, piece_of(late_a, x_from, p), own_send.at[0], late_recv.at[x_from, p], x_up).start()
+        remote(piece, piece_of(late_b, x_from, p), own_send.at[1], late_recv.at[2 + x_from, p], x_down).start()
 
         @pl.when(hub)
         def _():
@@ -193,24 +190,29 @@
         def _():
             meta_copy(meta_e.at[2], meta_e.at[4], 4, 5, beside).start()
 
-        def take(chunk, carry):
-            src = chunk_of(early, 1, chunk)
-            arrived(src, e1_recv.at[chunk])
-            remote(src, chunk_of(late, 0, chunk), fwd_send.at[0], late_recv.at[0, chunk], up).start()
-            remote(src, chunk_of(late, 1, chunk), fwd_send.at[1], late_recv.at[1, chunk], down).start()
+        def take(p, carry):
+            for q in range(PER):
+                chunk = p * PER + q
+                src = chunk_of(early, 2, chunk)
+                arrived(src, e2_recv.at[chunk])
+
+                @pl.when(is_b)
+                def _(src=src, chunk=chunk):
+                    remote(src, chunk_of(early, 4, chunk), own_send.at[4], one_recv.at[1], beside).start()
+
+            piece = piece_of(early, 1, p)
+            arrived(piece, e1_recv.at[p])
+            for q in range(PER):
+                chunk = p * PER + q
+                remote(chunk_of(early, 1, chunk), chunk_of(late_a, 0, chunk), fwd_send.at[0], l0_recv.at[chunk], up).start()
+            remote(piece, piece_of(late_a, 1, p), fwd_send.at[1], late_recv.at[1, p], down).start()
 
             @pl.when(is_a)
             def _():
-                remote(src, chunk_of(late, 2, chunk), fwd_send.at[2], late_recv.at[2, chunk], beside).start()
-
-            arrived(chunk_of(early, 2, chunk), e2_recv.at[chunk])
-
-            @pl.when(is_b)
-            def _():
-                remote(chunk_of(early, 2, chunk), chunk_of(early, 4, chunk), own_send.at[4], one_recv.at[1], beside).start()
+                remote(piece, piece_of(late_b, 0, p), fwd_send.at[2], late_recv.at[2, p], beside).start()
             return carry
 
-        lax.fori_loop(0, CHUNKS, take, 0)
+        lax.fori_loop(0, PIECES, take, 0)
         arrived(meta_l.at[0], meta_recv.at[LATE])
 
         @pl.when(is_b)
@@ -309,8 +311,9 @@
 
     def pair(kind, at):
         row, col, row_item, col_item, row_block, col_block, alive = look_up(kind, at)
-        row_ref, row_meta = (late, meta_l) if kind == 2 else (early, meta_e)
-        col_ref, col_meta = (late, meta_l) if kind > 0 else (early, meta_e)
+        row_ref, row_meta = (late_a, meta_l) if kind == 2 else (early, meta_e)
+        col_ref, col_meta = (late_a if at == 0 else late_b, meta_l) if kind == 2 else (early, meta_e)
+        col_at = col - 2 if kind == 2 and at > 0 else col
         rows = row_ref[row, row_block]
         row_labs = labels_down(row_meta, row, row_block)
         col_labs = [col_meta[col, col_block, i:i + 1, :].astype(jnp.float32) for i in range(4)]
@@ -321,7 +324,7 @@
             off = off | (jnp.full((128, 128), apart, jnp.int32) > 0)
         row_best, col_best = [None] * 4, []
         for n in range(2):
-            cols = col_ref[col, col_block, n * PIECE:(n + 1) * PIECE, :]
+            cols = col_ref[col_at, col_block, n * PIECE:(n + 1) * PIECE, :]
             score(rows, cols, row_labs, col_labs[2 * n:2 * n + 2], off, row_best, col_best)
         raise_best(row_item, down_rows(row_best), (block_at == row_block) & (full(alive) > 0))
         raise_best(col_item, jnp.concatenate(col_best * 4, axis=0), (block_at == col_block) & (full(alive) > 0))
@@ -333,47 +336,67 @@
         row_labs = labels_down(meta_e, row, row_block)
         col_labs = [meta_l[col, block, pl.ds(half * 2 + j, 1), :].astype(jnp.float32) for j in range(2)]
         row_best, col_best = [None] * 4, []
-        score(rows, piece_of(late, col, p)[...], row_labs, col_labs, None, row_best, col_best)
+        cols = piece_of(late_a, col, p) if at < EL_A else piece_of(late_b, col - 2, p)
+        score(rows, cols[...], row_labs, col_labs, None, row_best, col_best)
         asked = full(jnp.where(col_block == block, alive, 0)) > 0
         raise_best(row_item, down_rows(row_best), (block_at == row_block) & asked)
         at_line = block * 4 + half * 2
         both = jnp.where(line == at_line, col_best[0], col_best[1])
         raise_best(col_item, both, asked & ((line == at_line) | (line == at_line + 1)))
 
-    def pass_on(chunk):
-        src = chunk_of(late, 0, chunk)
-        arrived(src, late_recv.at[0, chunk])
-
-        @pl.when(is_b)
-        def _():
-            remote(src, chunk_of(late, 2, chunk), fwd_send.at[2], late_recv.at[2, chunk], beside).start()
-
-    early_pairs = len(EE_CLUS) + (len(EE_HUB) - len(EE_CLUS)) * hub_f
+    def pass_on(p, q):
+        chunk = p * PER + q
+
+        @pl.when(hub & (p < PIECES))
+        def _():
+            src = chunk_of(late_a, 0, chunk)
+            arrived(src, l0_recv.at[chunk])
+
+            @pl.when(is_b)
+            def _():
+                remote(src, chunk_of(late_b, 0, chunk), fwd_send.at[2], late_recv.at[2, p], beside).start()
+
+    early_pairs = len(EE_CLUS) + (len(EE_HUB) - 2 - len(EE_CLUS)) * hub_f
 
     def step(p, carry):
-        @pl.when(hub)
-        def _():
-            pass_on(2 * p)
+        pass_on(p, 0)
 
         @pl.when(2 * p < early_pairs)
         def _():
             pair(0, 2 * p)
             pair(0, 2 * p + 1)
 
-        @pl.when(hub)
-        def _():
-            pass_on(2 * p + 1)
-            for item in (1, 2):
-                for chunk in (2 * p, 2 * p + 1):
-                    arrived(chunk_of(late, item, chunk), late_recv.at[item, chunk])
-
-        @pl.when(hub_f == 0)
-        def _():
-            for item in range(4):
-                arrived(piece_of(late, item, p), late_recv.at[item, p])
-
-        for at in range(len(EL_HUB)):
-            late_pair(at, p)
+        pass_on(p, 1)
+
+        @pl.when(p > 0)
+        def _():
+            arrived(piece_of(late_a, 1, p - 1), late_recv.at[1, p - 1])
+
+            @pl.when(hub_f == 0)
+            def _():
+                arrived(piece_of(late_a, 0, p - 1), late_recv.at[0, p - 1])
+
+            for at in range(EL_A):
+                late_pair(at, p - 1)
+
+        pass_on(p, 2)
+
+        @pl.when(hub & (p == PIECES))
+        def _():
+            pair(2, 0)
+
+        @pl.when(p > 0)
+        def _():
+            arrived(piece_of(late_b, 0, p - 1), late_recv.at[2, p - 1])
+
+            @pl.when(hub_f == 0)
+            def _():
+                arrived(piece_of(late_b, 1, p - 1), late_recv.at[3, p - 1])
+
+            for at in range(EL_A, len(EL_HUB)):
+                late_pair(at, p - 1)
+
+        pass_on(p, 3)
         return carry
 
     @pl.when(hub)
@@ -381,9 +404,14 @@
         pair(0, 16)
         pair(0, 17)
 
-    lax.fori_loop(0, PIECES, step, 0)
-    for at in range(len(LL_HUB)):
-        pair(2, at)
+    lax.fori_loop(0, PIECES + 1, step, 0)
+    pair(2, 1)
+    pair(2, 2)
+
+    @pl.when(hub_f == 0)
+    def _():
+        pair(2, 3)
+        pair(2, 4)
 
     def give(item, to, send, device):
         return remote(best.at[item], ret.at[to], ret_send.at[send], ret_recv.at[to], device)
@@ -443,14 +471,15 @@
         out_specs=vmem,
         scratch_shapes=[
             pltpu.VMEM((5, BLOCKS, BLOCK, D), jnp.bfloat16),
-            pltpu.VMEM((4, BLOCKS, BLOCK, D), jnp.bfloat16),
+            pltpu.VMEM((2, BLOCKS, BLOCK, D), jnp.bfloat16),
+            pltpu.VMEM((2, BLOCKS, BLOCK, D), jnp.bfloat16),
             pltpu.VMEM((5, BLOCKS + 1, 8, 128), jnp.int32),
             pltpu.VMEM((4, BLOCKS + 1, 8, 128), jnp.int32),
             pltpu.SMEM((9, 8, 128), jnp.int32),
             pltpu.VMEM((9, 16, 128), jnp.float32),
             pltpu.VMEM((6, 16, 128), jnp.float32),
             dma((PIECES,)), dma((9,)), dma((6,)), dma((3,)), dma((9,)), dma((7,)),
-            dma((CHUNKS,)), dma((CHUNKS,)), dma((4, CHUNKS)), dma((3,)), dma((9,)), dma((6,)),
+            dma((PIECES,)), dma((CHUNKS,)), dma((CHUNKS,)), dma((4, PIECES)), dma((3,)), dma((9,)), dma((6,)),
         ],
         compiler_params=pltpu.CompilerParams(collective_id=0, has_side_effects=True, vmem_limit_bytes=56 << 20),
         cost_estimate=pl.CostEstimate(flops=24 * 2 * 512 * 512 * 1024, bytes_accessed=4 << 20, transcendentals=2048),

time: 118 us -> 115 us (0.975)
  Pallas kernels: 117 us -> 113 us
    pallas_call x1, Pallas kernels: 117 us -> 113 us  [on_device(): pl.pallas_call(kernel, out_shape=jax.ShapeDtypeStruct((16, 128), jnp.floa...]
where the time goes in v3:
time: 115 us
  Pallas kernels  113 us (98%)
  local copies, waits for them, and re-layouts  1.3 us (1%)
    pallas_call x1, Pallas kernels, on_device(): pl.pallas_call(kernel, out_shape=jax.ShapeDtypeStruct((16, 128), jnp.floa...  113 us

profile of v3, /device:TPU:1, one launch (start us, length us, event | category | flops | bytes accessed | tf_op | source)
XLA Modules:
  0.0 114.7 jit_solution(2929245477432870267)
XLA Ops:
  0.0 113.4 %shard_map.55 = f32[16,128]{1,0:T(8,128)} custom-call(bf16[2048,1024]{1,0:T(8,128)(2,1)} %emb.1, s32[16,128]{1,0:T(8,128)} %bitcast.3, s32[1,24]{1,0:T(1,128)} %own_tab.1, s32[1,24]{1,0:T(1,128)} %part_tab.1, s32[1,24]{1,0:T(1,128)} %live_tab.1), custom_call_target="tpu_custom_call" | custom-call | flops 12884901888 | bytes 4194304 | tf_op jit(solution)/shard_map/pallas_call | solution.py:467
  113.4 1.3 %copy.7 = f32[2048]{0:T(1024)} copy(f32[2048]{0:T(1024)} %bitcast.2) | data formatting | bytes 16384

commit v4 on v3

--- a/solution.py
+++ b/solution.py
@@ -47,7 +47,7 @@
     return sum(int(value) << at for at, value in enumerate(values))
 
 
-def kernel(emb, labs, own_tab, part_tab, live_tab, out, early, late_a, late_b, meta_e, meta_l, tabs, best, ret,
+def kernel(emb, labs_in, own_in, part_in, live_in, out, early, late_a, late_b, labs, small, meta_e, meta_l, tabs, best, ret,
            in_sem, tab_sem, own_send, fwd_send, meta_send, ret_send,
            e1_recv, e2_recv, l0_recv, late_recv, one_recv, meta_recv, ret_recv):
     c = lax.axis_index("clus")
@@ -95,12 +95,20 @@
     def piece_in(p):
         return pltpu.make_async_copy(emb.at[pl.ds(p * PIECE, PIECE)], piece_of(early, 0, p), in_sem.at[p])
 
-    for p in range(PIECES):
+    into = [pltpu.make_async_copy(labs_in, labs, in_sem.at[PIECES])]
+    into += [pltpu.make_async_copy(tab, small.at[at], in_sem.at[PIECES + 1 + at])
+             for at, tab in enumerate((own_in, part_in, live_in))]
+    piece_in(0).start()
+    for copy in into:
+        copy.start()
+    for p in range(1, PIECES):
         piece_in(p).start()
+    for copy in into:
+        copy.wait()
     for b in range(BLOCKS):
         meta_e[0, b, 0:4, :] = labs[4 * b:4 * b + 4, :]
-    for at, tab in enumerate((own_tab, part_tab, live_tab)):
-        meta_e[0, BLOCKS, at:at + 1, 0:24] = tab[...]
+    for at in range(3):
+        meta_e[0, BLOCKS, at:at + 1, 0:24] = small[at]
 
     def remote(src, dst, send, recv, device):
         return pltpu.make_async_remote_copy(src_ref=src, dst_ref=dst, send_sem=send, recv_sem=recv,
@@ -119,27 +127,11 @@
         inverse = lax.rsqrt(jnp.sum(wide * wide, axis=1, keepdims=True) + EPS)
         rows[...] = (wide * inverse).astype(jnp.bfloat16)
 
+    best[...] = jnp.full(best.shape, FILL, jnp.float32)
     normalize(0)
     pl.semaphore_wait(barrier, 3 + 3 * hub_f)
 
     x_from = 1 - hub_f
-    meta_copy(meta_e.at[0], meta_l.at[x_from], LATE + x_from, 0, x_up).start()
-    meta_copy(meta_e.at[0], meta_l.at[2 + x_from], LATE + 2 + x_from, 1, x_down).start()
-
-    @pl.when(hub)
-    def _():
-        meta_copy(meta_e.at[0], meta_e.at[2], 2, 2, up).start()
-        meta_copy(meta_e.at[0], meta_e.at[3], 3, 3, down).start()
-        meta_copy(meta_e.at[0], meta_e.at[1], 1, 4, mate).start()
-
-        @pl.when(is_a)
-        def _():
-            meta_copy(meta_e.at[0], meta_e.at[4], 4, 5, beside).start()
-
-    @pl.when(hub_f == 0)
-    def _():
-        meta_copy(meta_e.at[0], meta_e.at[1], 1, 2, beside).start()
-
     def send_own(p):
         piece = piece_of(early, 0, p)
 
@@ -165,14 +157,47 @@
         def _():
             remote(piece, piece_of(early, 1, p), own_send.at[5], one_recv.at[2], mate).start()
 
+    def across_early(chunk):
+        src = chunk_of(early, 2, chunk)
+        arrived(src, e2_recv.at[chunk])
+
+        @pl.when(is_b)
+        def _():
+            remote(src, chunk_of(early, 4, chunk), own_send.at[4], one_recv.at[1], beside).start()
+
+    meta_copy(meta_e.at[0], meta_l.at[x_from], LATE + x_from, 0, x_up).start()
+    meta_copy(meta_e.at[0], meta_l.at[2 + x_from], LATE + 2 + x_from, 1, x_down).start()
+
+    @pl.when(hub)
+    def _():
+        meta_copy(meta_e.at[0], meta_e.at[2], 2, 2, up).start()
+        meta_copy(meta_e.at[0], meta_e.at[3], 3, 3, down).start()
+        meta_copy(meta_e.at[0], meta_e.at[1], 1, 4, mate).start()
+
+        @pl.when(is_a)
+        def _():
+            meta_copy(meta_e.at[0], meta_e.at[4], 4, 5, beside).start()
+
+    @pl.when(hub_f == 0)
+    def _():
+        meta_copy(meta_e.at[0], meta_e.at[1], 1, 2, beside).start()
+
     send_own(0)
 
     def rest(p, carry):
         normalize(p)
         send_own(p)
+
+        @pl.when(hub & (p >= PIECES - PER))
+        def _():
+            across_early(p - (PIECES - PER))
         return carry
 
     lax.fori_loop(1, PIECES, rest, 0)
+
+    copies = [pltpu.make_async_copy(meta_e.at[item, BLOCKS], tabs.at[item], tab_sem.at[item]) for item in range(5)]
+    copies += [pltpu.make_async_copy(meta_l.at[item, BLOCKS], tabs.at[LATE + item], tab_sem.at[LATE + item])
+               for item in range(4)]
 
     @pl.when(hub)
     def _():
@@ -191,14 +216,10 @@
             meta_copy(meta_e.at[2], meta_e.at[4], 4, 5, beside).start()
 
         def take(p, carry):
-            for q in range(PER):
-                chunk = p * PER + q
-                src = chunk_of(early, 2, chunk)
-                arrived(src, e2_recv.at[chunk])
-
-                @pl.when(is_b)
-                def _(src=src, chunk=chunk):
-                    remote(src, chunk_of(early, 4, chunk), own_send.at[4], one_recv.at[1], beside).start()
+            @pl.when(p < PIECES - 1)
+            def _():
+                for q in range(PER):
+                    across_early((p + 1) * PER + q)
 
             piece = piece_of(early, 1, p)
             arrived(piece, e1_recv.at[p])
@@ -219,29 +240,16 @@
         def _():
             meta_copy(meta_l.at[0], meta_l.at[2], LATE + 2, 8, beside).start()
 
-        arrived(early.at[3], one_recv.at[0])
-        arrived(early.at[4], one_recv.at[1])
-        for item in (3, 4):
-            arrived(meta_e.at[item], meta_recv.at[item])
-        for item in (1, 2):
-            arrived(meta_l.at[item], meta_recv.at[LATE + item])
-
     @pl.when(hub_f == 0)
     def _():
         arrived(early.at[1], one_recv.at[2])
         arrived(meta_e.at[1], meta_recv.at[1])
         for item in range(4):
             arrived(meta_l.at[item], meta_recv.at[LATE + item])
-
-    copies = [pltpu.make_async_copy(meta_e.at[item, BLOCKS], tabs.at[item], tab_sem.at[item]) for item in range(5)]
-    copies += [pltpu.make_async_copy(meta_l.at[item, BLOCKS], tabs.at[LATE + item], tab_sem.at[LATE + item])
-               for item in range(4)]
-    for copy in copies:
-        copy.start()
-    for copy in copies:
-        copy.wait()
-
-    best[...] = jnp.full(best.shape, FILL, jnp.float32)
+        for copy in copies:
+            copy.start()
+        for copy in copies:
+            copy.wait()
 
     def by_role(for_hub, for_clus):
         return for_clus + (for_hub - for_clus) * hub_f
@@ -347,7 +355,7 @@
     def pass_on(p, q):
         chunk = p * PER + q
 
-        @pl.when(hub & (p < PIECES))
+        @pl.when(hub)
         def _():
             src = chunk_of(late_a, 0, chunk)
             arrived(src, l0_recv.at[chunk])
@@ -358,9 +366,42 @@
 
     early_pairs = len(EE_CLUS) + (len(EE_HUB) - 2 - len(EE_CLUS)) * hub_f
 
+    def late_a_pairs(p):
+        arrived(piece_of(late_a, 1, p), late_recv.at[1, p])
+
+        @pl.when(hub_f == 0)
+        def _():
+            arrived(piece_of(late_a, 0, p), late_recv.at[0, p])
+
+        for at in range(EL_A):
+            late_pair(at, p)
+
+    def late_b_pairs(p):
+        arrived(piece_of(late_b, 0, p), late_recv.at[2, p])
+
+        @pl.when(hub_f == 0)
+        def _():
+            arrived(piece_of(late_b, 1, p), late_recv.at[3, p])
+
+        for at in range(EL_A, len(EL_HUB)):
+            late_pair(at, p)
+
     def step(p, carry):
         pass_on(p, 0)
 
+        @pl.when(hub & (p == 0))
+        def _():
+            arrived(early.at[3], one_recv.at[0])
+            arrived(early.at[4], one_recv.at[1])
+            for item in (3, 4):
+                arrived(meta_e.at[item], meta_recv.at[item])
+            for item in (1, 2):
+                arrived(meta_l.at[item], meta_recv.at[LATE + item])
+            for copy in copies:
+                copy.start()
+            for copy in copies:
+                copy.wait()
+
         @pl.when(2 * p < early_pairs)
         def _():
             pair(0, 2 * p)
@@ -370,43 +411,27 @@
 
         @pl.when(p > 0)
         def _():
-            arrived(piece_of(late_a, 1, p - 1), late_recv.at[1, p - 1])
-
-            @pl.when(hub_f == 0)
-            def _():
-                arrived(piece_of(late_a, 0, p - 1), late_recv.at[0, p - 1])
-
-            for at in range(EL_A):
-                late_pair(at, p - 1)
+            late_a_pairs(p - 1)
+
+        @pl.when(hub & (p == 0))
+        def _():
+            pair(0, 16)
+            pair(0, 17)
 
         pass_on(p, 2)
 
-        @pl.when(hub & (p == PIECES))
-        def _():
-            pair(2, 0)
-
         @pl.when(p > 0)
         def _():
-            arrived(piece_of(late_b, 0, p - 1), late_recv.at[2, p - 1])
-
-            @pl.when(hub_f == 0)
-            def _():
-                arrived(piece_of(late_b, 1, p - 1), late_recv.at[3, p - 1])
-
-            for at in range(EL_A, len(EL_HUB)):
-                late_pair(at, p - 1)
+            late_b_pairs(p - 1)
 
         pass_on(p, 3)
         return carry
 
-    @pl.when(hub)
-    def _():
-        pair(0, 16)
-        pair(0, 17)
-
-    lax.fori_loop(0, PIECES + 1, step, 0)
-    pair(2, 1)
-    pair(2, 2)
+    lax.fori_loop(0, PIECES, step, 0)
+    late_a_pairs(PIECES - 1)
+    late_b_pairs(PIECES - 1)
+    for at in range(3):
+        pair(2, at)
 
     @pl.when(hub_f == 0)
     def _():
@@ -429,7 +454,7 @@
     for which, gives in ((is_a, lambda: hub_gives(True)), (is_b, lambda: hub_gives(False)), (hub_f == 0, clus_gives)):
         @pl.when(which)
         def _(gives=gives):
-            for copy in gives():
+            for copy in reversed(gives()):
                 copy.start()
 
     for s in range(2):
@@ -467,18 +492,20 @@
     best = pl.pallas_call(
         kernel,
         out_shape=jax.ShapeDtypeStruct((16, 128), jnp.float32),
-        in_specs=[pl.BlockSpec(memory_space=pl.ANY), vmem, vmem, vmem, vmem],
+        in_specs=[pl.BlockSpec(memory_space=pl.ANY)] * 5,
         out_specs=vmem,
         scratch_shapes=[
             pltpu.VMEM((5, BLOCKS, BLOCK, D), jnp.bfloat16),
             pltpu.VMEM((2, BLOCKS, BLOCK, D), jnp.bfloat16),
             pltpu.VMEM((2, BLOCKS, BLOCK, D), jnp.bfloat16),
+            pltpu.VMEM((16, 128), jnp.int32),
+            pltpu.VMEM((3, 1, 24), jnp.int32),
             pltpu.VMEM((5, BLOCKS + 1, 8, 128), jnp.int32),
             pltpu.VMEM((4, BLOCKS + 1, 8, 128), jnp.int32),
             pltpu.SMEM((9, 8, 128), jnp.int32),
             pltpu.VMEM((9, 16, 128), jnp.float32),
             pltpu.VMEM((6, 16, 128), jnp.float32),
-            dma((PIECES,)), dma((9,)), dma((6,)), dma((3,)), dma((9,)), dma((7,)),
+            dma((PIECES + 4,)), dma((9,)), dma((6,)), dma((3,)), dma((9,)), dma((7,)),
             dma((PIECES,)), dma((CHUNKS,)), dma((CHUNKS,)), dma((4, PIECES)), dma((3,)), dma((9,)), dma((6,)),
         ],
         compiler_params=pltpu.CompilerParams(collective_id=0, has_side_effects=True, vmem_limit_bytes=56 << 20),

time: 115 us -> 114 us (level)
    pallas_call x1, Pallas kernels: 113 us -> 112 us  [on_device(): pl.pallas_call(kernel, out_shape=jax.ShapeDtypeStruct((16, 128), jnp.floa...]
where the time goes in v4:
time: 114 us; the launch traced here: 113 us
  Pallas kernels  112 us (98%)
  local copies, waits for them, and re-layouts  1.3 us (1%)
    pallas_call x1, Pallas kernels, on_device(): pl.pallas_call(kernel, out_shape=jax.ShapeDtypeStruct((16, 128), jnp.floa...  112 us

profile of v4, /device:TPU:1, one launch (start us, length us, event | category | flops | bytes accessed | tf_op | source)
XLA Modules:
  0.0 113.4 jit_solution(12404478714990198287)
XLA Ops:
  0.0 112.1 %shard_map.55 = f32[16,128]{1,0:T(8,128)} custom-call(bf16[2048,1024]{1,0:T(8,128)(2,1)} %emb.1, s32[16,128]{1,0:T(8,128)} %bitcast.3, s32[1,24]{1,0:T(1,128)} %own_in.1, s32[1,24]{1,0:T(1,128)} %part_in.1, s32[1,24]{1,0:T(1,128)} %live_in.1), custom_call_target="tpu_custom_call" | custom-call | flops 12884901888 | bytes 4194304 | tf_op jit(solution)/shard_map/pallas_call | solution.py:492
  112.2 1.3 %copy.7 = f32[2048]{0:T(1024)} copy(f32[2048]{0:T(1024)} %bitcast.2) | data formatting | bytes 16384

commit v5 on v4

--- a/solution.py
+++ b/solution.py
@@ -15,9 +15,10 @@
 
 PIECE = 256
 PIECES = ROWS // PIECE
-CHUNK = 64
-CHUNKS = ROWS // CHUNK
-PER = PIECE // CHUNK
+PER = 4
+CHUNKS = PIECES * PER
+WIDTH = D // PER
+HALF = D // 2
 
 EE_HUB = [(0, 0, 0), (0, 0, 0), (0, 1, 0), (0, 1, 1), (0, 2, 0), (0, 3, 0), (2, 3, 0), (1, 2, 0), (1, 2, 1),
           (1, 3, 0), (1, 3, 1), (0, 4, 0), (0, 4, 1), (1, 4, 0), (1, 4, 1), (3, 4, 0), (3, 4, 1), (3, 4, 1)]
@@ -47,7 +48,7 @@
     return sum(int(value) << at for at, value in enumerate(values))
 
 
-def kernel(emb, labs_in, own_in, part_in, live_in, out, early, late_a, late_b, labs, small, meta_e, meta_l, tabs, best, ret,
+def kernel(emb, labs_in, own_in, part_in, live_in, out, early, late_a, late_b, labs, small, meta_e, meta_l, tabs, best, part, ret,
            in_sem, tab_sem, own_send, fwd_send, meta_send, ret_send,
            e1_recv, e2_recv, l0_recv, late_recv, one_recv, meta_recv, ret_recv):
     c = lax.axis_index("clus")
@@ -89,8 +90,15 @@
     def piece_of(ref, item, p):
         return part_of(ref, item, p, PIECE)
 
+    def slab_of(ref, item, p, first, width):
+        rows = pl.ds(pl.multiple_of(p % 2 * PIECE, PIECE), PIECE)
+        return ref.at[item, p // 2, rows, pl.ds(pl.multiple_of(first, width), width)]
+
     def chunk_of(ref, item, chunk):
-        return part_of(ref, item, chunk, CHUNK)
+        return slab_of(ref, item, chunk // PER, chunk % PER * WIDTH, WIDTH)
+
+    def half_of(ref, item, p, h):
+        return slab_of(ref, item, p, h * HALF, HALF)
 
     def piece_in(p):
         return pltpu.make_async_copy(emb.at[pl.ds(p * PIECE, PIECE)], piece_of(early, 0, p), in_sem.at[p])
@@ -150,8 +158,10 @@
         def _():
             remote(piece, piece_of(early, 1, p), own_send.at[2], e1_recv.at[p], beside).start()
 
-        remote(piece, piece_of(late_a, x_from, p), own_send.at[0], late_recv.at[x_from, p], x_up).start()
-        remote(piece, piece_of(late_b, x_from, p), own_send.at[1], late_recv.at[2 + x_from, p], x_down).start()
+        for h in range(2):
+            src = half_of(early, 0, p, h)
+            remote(src, half_of(late_a, x_from, p, h), own_send.at[0], late_recv.at[x_from, p, h], x_up).start()
+            remote(src, half_of(late_b, x_from, p, h), own_send.at[1], late_recv.at[2 + x_from, p, h], x_down).start()
 
         @pl.when(hub)
         def _():
@@ -226,11 +236,15 @@
             for q in range(PER):
                 chunk = p * PER + q
                 remote(chunk_of(early, 1, chunk), chunk_of(late_a, 0, chunk), fwd_send.at[0], l0_recv.at[chunk], up).start()
-            remote(piece, piece_of(late_a, 1, p), fwd_send.at[1], late_recv.at[1, p], down).start()
+            for h in range(2):
+                src = half_of(early, 1, p, h)
+                remote(src, half_of(late_a, 1, p, h), fwd_send.at[1], late_recv.at[1, p, h], down).start()
 
             @pl.when(is_a)
             def _():
-                remote(piece, piece_of(late_b, 0, p), fwd_send.at[2], late_recv.at[2, p], beside).start()
+                for h in range(2):
+                    src = half_of(early, 1, p, h)
+                    remote(src, half_of(late_b, 0, p, h), fwd_send.at[2], late_recv.at[2, p, h], beside).start()
             return carry
 
         lax.fori_loop(0, PIECES, take, 0)
@@ -299,8 +313,10 @@
     def full(scalar):
         return jnp.full((16, 128), scalar, jnp.int32)
 
-    def score(rows, cols, row_labs, col_labs, off, row_best, col_best):
-        cosine = lax.dot_general(rows, cols, (((1,), (1,)), ((), ())), preferred_element_type=jnp.float32)
+    def product(rows, cols):
+        return lax.dot_general(rows, cols, (((1,), (1,)), ((), ())), preferred_element_type=jnp.float32)
+
+    def score(cosine, row_labs, col_labs, off, row_best, col_best):
         for j, col_lab in enumerate(col_labs):
             line_best = None
             for i in range(4):
@@ -333,25 +349,39 @@
         row_best, col_best = [None] * 4, []
         for n in range(2):
             cols = col_ref[col_at, col_block, n * PIECE:(n + 1) * PIECE, :]
-            score(rows, cols, row_labs, col_labs[2 * n:2 * n + 2], off, row_best, col_best)
+            score(product(rows, cols), row_labs, col_labs[2 * n:2 * n + 2], off, row_best, col_best)
         raise_best(row_item, down_rows(row_best), (block_at == row_block) & (full(alive) > 0))
         raise_best(col_item, jnp.concatenate(col_best * 4, axis=0), (block_at == col_block) & (full(alive) > 0))
 
-    def late_pair(at, p):
+    def first_half(at, p):
+        row, col, _, _, row_block, _, _ = look_up(1, at)
+        cols = half_of(late_a, col, p, 0) if at < EL_A else half_of(late_b, col - 2, p, 0)
+        part[at] = product(early[row, row_block, :, :HALF], cols[...])
+
+    def late_pair(at, p, halved=False):
         row, col, row_item, col_item, row_block, col_block, alive = look_up(1, at)
         block, half = p // 2, p % 2
-        rows = early[row, row_block]
         row_labs = labels_down(meta_e, row, row_block)
         col_labs = [meta_l[col, block, pl.ds(half * 2 + j, 1), :].astype(jnp.float32) for j in range(2)]
         row_best, col_best = [None] * 4, []
-        cols = piece_of(late_a, col, p) if at < EL_A else piece_of(late_b, col - 2, p)
-        score(rows, cols[...], row_labs, col_labs, None, row_best, col_best)
+        late, late_at = (late_a, col) if at < EL_A else (late_b, col - 2)
+        if halved:
+            cosine = part[at] + product(early[row, row_block, :, HALF:], half_of(late, late_at, p, 1)[...])
+        else:
+            cosine = product(early[row, row_block], piece_of(late, late_at, p)[...])
+        score(cosine, row_labs, col_labs, None, row_best, col_best)
         asked = full(jnp.where(col_block == block, alive, 0)) > 0
         raise_best(row_item, down_rows(row_best), (block_at == row_block) & asked)
         at_line = block * 4 + half * 2
         both = jnp.where(line == at_line, col_best[0], col_best[1])
         raise_best(col_item, both, asked & ((line == at_line) | (line == at_line + 1)))
 
+    in_b = yy % 2
+    aside = 3 - 2 * in_b
+    hub_owners = [(0, dev(0, k, 0, aside)), (0, dev(0, k, 3, 0)), (1, dev(0, k, 1, 0)),
+                  (2, dev(0, k, 3 - 3 * in_b, 1 + 2 * in_b)), (1, dev(0, k, 3, aside)), (2, dev(0, k, 1, aside)),
+                  (3, dev(0, k, 3 - 3 * in_b, 2))]
+
     def pass_on(p, q):
         chunk = p * PER + q
 
@@ -362,27 +392,33 @@
 
             @pl.when(is_b)
             def _():
-                remote(src, chunk_of(late_b, 0, chunk), fwd_send.at[2], late_recv.at[2, p], beside).start()
-
-    early_pairs = len(EE_CLUS) + (len(EE_HUB) - 2 - len(EE_CLUS)) * hub_f
+                remote(src, chunk_of(late_b, 0, chunk), fwd_send.at[2], late_recv.at[2, p, q // 2], beside).start()
+
+    early_pairs = len(EE_CLUS) + (len(EE_HUB) - 4 - len(EE_CLUS)) * hub_f
+
+    def late_a_landed(p, h):
+        arrived(half_of(late_a, 1, p, h), late_recv.at[1, p, h])
+
+        @pl.when(hub_f == 0)
+        def _():
+            arrived(half_of(late_a, 0, p, h), late_recv.at[0, p, h])
+
+    def late_b_landed(p, h):
+        arrived(half_of(late_b, 0, p, h), late_recv.at[2, p, h])
+
+        @pl.when(hub_f == 0)
+        def _():
+            arrived(half_of(late_b, 1, p, h), late_recv.at[3, p, h])
 
     def late_a_pairs(p):
-        arrived(piece_of(late_a, 1, p), late_recv.at[1, p])
-
-        @pl.when(hub_f == 0)
-        def _():
-            arrived(piece_of(late_a, 0, p), late_recv.at[0, p])
-
+        for h in range(2):
+            late_a_landed(p, h)
         for at in range(EL_A):
             late_pair(at, p)
 
     def late_b_pairs(p):
-        arrived(piece_of(late_b, 0, p), late_recv.at[2, p])
-
-        @pl.when(hub_f == 0)
-        def _():
-            arrived(piece_of(late_b, 1, p), late_recv.at[3, p])
-
+        for h in range(2):
+            late_b_landed(p, h)
         for at in range(EL_A, len(EL_HUB)):
             late_pair(at, p)
 
@@ -424,12 +460,34 @@
         def _():
             late_b_pairs(p - 1)
 
+        @pl.when(hub & (p == 0))
+        def _():
+            pair(0, 14)
+            pair(0, 15)
+
         pass_on(p, 3)
         return carry
 
-    lax.fori_loop(0, PIECES, step, 0)
-    late_a_pairs(PIECES - 1)
-    late_b_pairs(PIECES - 1)
+    lax.fori_loop(0, PIECES - 1, step, 0)
+    last = PIECES - 1
+    pass_on(last, 0)
+    late_a_pairs(last - 1)
+    pass_on(last, 1)
+    late_b_pairs(last - 1)
+    pass_on(last, 2)
+    late_a_landed(last, 0)
+    for at in range(EL_A):
+        first_half(at, last)
+    pass_on(last, 3)
+    late_b_landed(last, 0)
+    for at in range(EL_A, len(EL_HUB)):
+        first_half(at, last)
+    late_a_landed(last, 1)
+    for at in range(EL_A):
+        late_pair(at, last, True)
+    late_b_landed(last, 1)
+    for at in range(EL_A, len(EL_HUB)):
+        late_pair(at, last, True)
     for at in range(3):
         pair(2, at)
 
@@ -441,17 +499,14 @@
     def give(item, to, send, device):
         return remote(best.at[item], ret.at[to], ret_send.at[send], ret_recv.at[to], device)
 
-    def hub_gives(a):
-        return [give(1, 0, 0, dev(0, k, 0, 3 if a else 1)), give(2, 0, 1, dev(0, k, 3, 0)), give(3, 1, 2, dev(0, k, 1, 0)),
-                give(4, 2, 3, dev(0, k, 3, 1) if a else dev(0, k, 0, 3)),
-                give(5, 1, 4, dev(0, k, 3, 3 if a else 1)), give(6, 2, 5, dev(0, k, 1, 3 if a else 1)),
-                give(7, 3, 6, dev(0, k, 3, 2) if a else dev(0, k, 0, 2))]
+    def hub_gives():
+        return [give(item, to, item - 1, device) for item, (to, device) in enumerate(hub_owners, 1)]
 
     def clus_gives():
         return [give(1, 3, 0, mate), give(5, 4, 1, dev(3, 1 - k, 0, 0)), give(6, 4, 2, dev(3, k, 0, 0)),
                 give(7, 5, 3, dev(1, 1 - k, 0, 0)), give(8, 5, 4, dev(1, k, 0, 0))]
 
-    for which, gives in ((is_a, lambda: hub_gives(True)), (is_b, lambda: hub_gives(False)), (hub_f == 0, clus_gives)):
+    for which, gives in ((hub, hub_gives), (hub_f == 0, clus_gives)):
         @pl.when(which)
         def _(gives=gives):
             for copy in reversed(gives()):
@@ -504,9 +559,10 @@
             pltpu.VMEM((4, BLOCKS + 1, 8, 128), jnp.int32),
             pltpu.SMEM((9, 8, 128), jnp.int32),
             pltpu.VMEM((9, 16, 128), jnp.float32),
+            pltpu.VMEM((len(EL_HUB), BLOCK, PIECE), jnp.float32),
             pltpu.VMEM((6, 16, 128), jnp.float32),
             dma((PIECES + 4,)), dma((9,)), dma((6,)), dma((3,)), dma((9,)), dma((7,)),
-            dma((PIECES,)), dma((CHUNKS,)), dma((CHUNKS,)), dma((4, PIECES)), dma((3,)), dma((9,)), dma((6,)),
+            dma((PIECES,)), dma((CHUNKS,)), dma((CHUNKS,)), dma((4, PIECES, 2)), dma((3,)), dma((9,)), dma((6,)),
         ],
         compiler_params=pltpu.CompilerParams(collective_id=0, has_side_effects=True, vmem_limit_bytes=56 << 20),
         cost_estimate=pl.CostEstimate(flops=24 * 2 * 512 * 512 * 1024, bytes_accessed=4 << 20, transcendentals=2048),

time: 114 us -> 113 us (level)
  no operation moved by 1% of the time
where the time goes in v5:
time: 113 us
  Pallas kernels  112 us (99%)
  local copies, waits for them, and re-layouts  1.3 us (1%)
    pallas_call x1, Pallas kernels, on_device(): pl.pallas_call(kernel, out_shape=jax.ShapeDtypeStruct((16, 128), jnp.floa...  112 us

profile of v5, /device:TPU:1, one launch (start us, length us, event | category | flops | bytes accessed | tf_op | source)
XLA Modules:
  0.0 113.3 jit_solution(17550895706788646777)
XLA Ops:
  0.0 112.0 %shard_map.55 = f32[16,128]{1,0:T(8,128)} custom-call(bf16[2048,1024]{1,0:T(8,128)(2,1)} %emb.1, s32[16,128]{1,0:T(8,128)} %bitcast.3, s32[1,24]{1,0:T(1,128)} %own_in.1, s32[1,24]{1,0:T(1,128)} %part_in.1, s32[1,24]{1,0:T(1,128)} %live_in.1), custom_call_target="tpu_custom_call" | custom-call | flops 12884901888 | bytes 4194304 | tf_op jit(solution)/shard_map/pallas_call | solution.py:547
  112.0 1.3 %copy.7 = f32[2048]{0:T(1024)} copy(f32[2048]{0:T(1024)} %bitcast.2) | data formatting | bytes 16384

commit v6 on v5

--- a/solution.py
+++ b/solution.py
@@ -485,10 +485,11 @@
     late_a_landed(last, 1)
     for at in range(EL_A):
         late_pair(at, last, True)
+    pair(2, 0)
     late_b_landed(last, 1)
     for at in range(EL_A, len(EL_HUB)):
         late_pair(at, last, True)
-    for at in range(3):
+    for at in range(1, 3):
         pair(2, at)
 
     @pl.when(hub_f == 0)

time: 113 us -> 113 us (level)
  no operation moved by 1% of the time
where the time goes in v6:
time: 113 us
  Pallas kernels  112 us (99%)
  local copies, waits for them, and re-layouts  1.3 us (1%)
    pallas_call x1, Pallas kernels, on_device(): pl.pallas_call(kernel, out_shape=jax.ShapeDtypeStruct((16, 128), jnp.floa...  112 us

profile of v6, /device:TPU:1, one launch (start us, length us, event | category | flops | bytes accessed | tf_op | source)
XLA Modules:
  0.0 113.3 jit_solution(13111825469365366054)
XLA Ops:
  0.0 112.0 %shard_map.55 = f32[16,128]{1,0:T(8,128)} custom-call(bf16[2048,1024]{1,0:T(8,128)(2,1)} %emb.1, s32[16,128]{1,0:T(8,128)} %bitcast.3, s32[1,24]{1,0:T(1,128)} %own_in.1, s32[1,24]{1,0:T(1,128)} %part_in.1, s32[1,24]{1,0:T(1,128)} %live_in.1), custom_call_target="tpu_custom_call" | custom-call | flops 12884901888 | bytes 4194304 | tf_op jit(solution)/shard_map/pallas_call | solution.py:548
  112.0 1.3 %copy.7 = f32[2048]{0:T(1024)} copy(f32[2048]{0:T(1024)} %bitcast.2) | data formatting | bytes 16384
